TPU v7x, 128 devices: a whole 4x4x4 slice. The times are simulated.
128 devices in a mesh: prow: 8 (over z, core), pcol: 8 (over y_hi, x), orb: 2 (over y_lo).
Axes of the slice: x: 4, y: 4 (y_hi: 2, y_lo: 2; y = y_hi * 2 + y_lo), z: 4, core: 2. Of those that a mesh axis runs over, the one named last changes fastest.
Arguments:
- g2_re: float32 [4096, 4096], P('prow', ('pcol', 'orb')), may hold values from -1 to 1
- g2_im: float32 [4096, 4096], P('prow', ('pcol', 'orb')), may hold values from -1 to 1
- g1_re: float32 [64, 64], P('prow', ('pcol', 'orb')), may hold values from -3 to 3
- g1_im: float32 [64, 64], P('prow', ('pcol', 'orb')), may hold values from -3 to 3
- hop_re: float32 [64, 64], replicated, may hold values from -0.75 to 0.75
- hop_im: float32 [64, 64], replicated, may hold values from -0.75 to 0.75
- coupling: float32 [64, 64], replicated, may hold values from 0.2 to 1.5
Outputs:
- dg2_re: float32 [4096, 4096], P('prow', ('pcol', 'orb'))
- dg2_im: float32 [4096, 4096], P('prow', ('pcol', 'orb'))
- dg1_re: float32 [64, 64], replicated
- dg1_im: float32 [64, 64], replicated
All inputs are finite; a program needn't handle non-finite values.
Results may differ from a plain program's by a relative error of at most 0.000076.
Values sent between devices are 32-bit elements; how exact they have to be, the bound alone decides.
A program may use at most 192 MiB of HBM per device.

v0:
```python
import jax
import jax.numpy as jnp
from jax import lax
from jax.sharding import PartitionSpec as P

HIGH = lax.Precision.HIGHEST


def hermitian(hop_re, hop_im):
    return (0.5 * (hop_re + hop_re.T), 0.5 * (hop_im - hop_im.T))


def contract(form, left_re, left_im, right_re, right_im):
    real_part = jnp.einsum(form, left_re, right_re, precision=HIGH) - jnp.einsum(
        form, left_im, right_im, precision=HIGH
    )
    imag_part = jnp.einsum(form, left_re, right_im, precision=HIGH) + jnp.einsum(
        form, left_im, right_re, precision=HIGH
    )
    return (real_part, imag_part)


def assemble(blocks, orbits, row_orbs, col_orbs):
    shaped = blocks.reshape(orbits // row_orbs, orbits // col_orbs, row_orbs, col_orbs)
    return shaped.transpose(0, 2, 1, 3).reshape(orbits, orbits)


def to_hole(block, row_orbs, orbits, col_orbs):
    shaped = block.reshape(row_orbs, orbits, col_orbs, orbits)
    return shaped.transpose(0, 3, 2, 1).reshape(row_orbs * orbits, col_orbs * orbits)


def on_device(g2_re, g2_im, g1_re, g1_im, hop_re, hop_im, coupling):
    orbits = hop_re.shape[0]
    pairs_all = orbits * orbits
    row_count, col_count = g2_re.shape
    row_orbs = row_count // orbits
    col_orbs = col_count // orbits
    row_index = lax.axis_index("prow")
    col_index = lax.axis_index(("pcol", "orb"))
    field_re, field_im = hermitian(hop_re, hop_im)
    flat_parts = (
        g1_re.reshape(1, row_orbs * g1_re.shape[1]),
        g1_im.reshape(1, row_orbs * g1_im.shape[1]),
    )
    gathered_re, gathered_im = (
        lax.all_gather(flat_parts[0], ("prow", "pcol", "orb"), axis=0, tiled=True),
        lax.all_gather(flat_parts[1], ("prow", "pcol", "orb"), axis=0, tiled=True),
    )
    whole_re = assemble(gathered_re, orbits, row_orbs, col_orbs)
    whole_im = assemble(gathered_im, orbits, row_orbs, col_orbs)
    hartree = jnp.dot(coupling, jnp.diagonal(whole_re), precision=HIGH)
    field_re = field_re + jnp.diag(hartree)
    hole_re = to_hole(g2_re, row_orbs, orbits, col_orbs)
    hole_im = to_hole(g2_im, row_orbs, orbits, col_orbs)
    identity = jnp.eye(orbits, dtype=jnp.float32)
    rows_re = lax.dynamic_slice_in_dim(field_re, row_index * row_orbs, row_orbs, 0)
    rows_im = lax.dynamic_slice_in_dim(field_im, row_index * row_orbs, row_orbs, 0)
    column_re, column_im = (
        lax.all_gather(hole_re, "prow", axis=0, tiled=True),
        lax.all_gather(hole_im, "prow", axis=0, tiled=True),
    )
    field_cols_re = lax.dynamic_slice_in_dim(field_re, col_index * col_orbs, col_orbs, 1)
    field_cols_im = lax.dynamic_slice_in_dim(field_im, col_index * col_orbs, col_orbs, 1)
    weights = coupling.reshape(pairs_all, 1)
    mixing_re = jnp.einsum("qk,bj->qbkj", field_cols_re, identity).reshape(pairs_all, col_count)
    mixing_im = jnp.einsum("qk,bj->qbkj", field_cols_im, identity).reshape(pairs_all, col_count)
    right_re = weights * column_re - mixing_re
    right_im = weights * column_im - mixing_im
    piece_re = lax.all_gather(hole_re, ("pcol", "orb"), axis=1, tiled=True)
    piece_im = lax.all_gather(hole_im, ("pcol", "orb"), axis=1, tiled=True)
    new_re = jnp.dot(piece_re, right_re, precision=HIGH) - jnp.dot(
        piece_im, right_im, precision=HIGH
    )
    new_im = jnp.dot(piece_re, right_im, precision=HIGH) + jnp.dot(
        piece_im, right_re, precision=HIGH
    )
    stack_re = column_re.reshape(orbits, orbits, col_count)
    stack_im = column_im.reshape(orbits, orbits, col_count)
    major_re, major_im = contract("ip,plc->ilc", rows_re, rows_im, stack_re, stack_im)
    joined_re = new_re + major_re.reshape(row_count, col_count)
    joined_im = new_im + major_im.reshape(row_count, col_count)
    paired_re = to_hole(joined_re, row_orbs, orbits, col_orbs).reshape(
        row_orbs, orbits, col_orbs, orbits
    )
    paired_im = to_hole(joined_im, row_orbs, orbits, col_orbs).reshape(
        row_orbs, orbits, col_orbs, orbits
    )
    tensor_re = g2_re.reshape(row_orbs, orbits, col_orbs, orbits)
    tensor_im = g2_im.reshape(row_orbs, orbits, col_orbs, orbits)
    minor_left = contract("jp,ipkl->ijkl", field_re, field_im, tensor_re, tensor_im)
    minor_right = contract("ijkq,ql->ijkl", tensor_re, tensor_im, field_re, field_im)
    coupling_rows = lax.dynamic_slice_in_dim(coupling, row_index * row_orbs, row_orbs, 0)
    coupling_cols = lax.dynamic_slice_in_dim(coupling, col_index * col_orbs, col_orbs, 0)
    spread = coupling_rows[:, :, None, None] - coupling_cols[None, None, :, :]
    total_re = paired_re + minor_left[0] - minor_right[0] + spread * tensor_re
    total_im = paired_im + minor_left[1] - minor_right[1] + spread * tensor_im
    dg2_re = total_im.reshape(row_count, col_count)
    dg2_im = -total_re.reshape(row_count, col_count)
    diagonal_re = jnp.diagonal(tensor_re, axis1=1, axis2=3)
    diagonal_im = jnp.diagonal(tensor_im, axis1=1, axis2=3)
    source_re = jnp.einsum("ijk,ik->ij", diagonal_re, coupling_rows, precision=HIGH)
    source_im = jnp.einsum("ijk,ik->ij", diagonal_im, coupling_rows, precision=HIGH)
    collide_parts = (
        source_im.reshape(1, row_orbs * col_orbs),
        (-source_re).reshape(1, row_orbs * col_orbs),
    )
    collide_all_re, collide_all_im = (
        lax.all_gather(collide_parts[0], ("prow", "pcol", "orb"), axis=0, tiled=True),
        lax.all_gather(collide_parts[1], ("prow", "pcol", "orb"), axis=0, tiled=True),
    )
    collide_re = assemble(collide_all_re, orbits, row_orbs, col_orbs)
    collide_im = assemble(collide_all_im, orbits, row_orbs, col_orbs)
    left_re = jnp.dot(field_re, whole_re, precision=HIGH) - jnp.dot(
        field_im, whole_im, precision=HIGH
    )
    left_im = jnp.dot(field_re, whole_im, precision=HIGH) + jnp.dot(
        field_im, whole_re, precision=HIGH
    )
    right_side_re = jnp.dot(whole_re, field_re, precision=HIGH) - jnp.dot(
        whole_im, field_im, precision=HIGH
    )
    right_side_im = jnp.dot(whole_re, field_im, precision=HIGH) + jnp.dot(
        whole_im, field_re, precision=HIGH
    )
    commute_re = left_re - right_side_re
    commute_im = left_im - right_side_im
    dg1_re = commute_im + collide_re + collide_re.T
    dg1_im = -commute_re + collide_im - collide_im.T
    return (dg2_re, dg2_im, dg1_re, dg1_im)


def solution(mesh):
    in_specs = (
        P("prow", ("pcol", "orb")),
        P("prow", ("pcol", "orb")),
        P("prow", ("pcol", "orb")),
        P("prow", ("pcol", "orb")),
        P(),
        P(),
        P(),
    )
    out_specs = (P("prow", ("pcol", "orb")), P("prow", ("pcol", "orb")), P(), P())
    return jax.shard_map(
        on_device, mesh=mesh, in_specs=in_specs, out_specs=out_specs, check_vma=False
    )
```

profile of v0, /device:TPU:0, one launch (start us, length us, event | category | flops | bytes accessed | tf_op | source)
XLA Modules:
  0.0 1433.6 jit_solution(17329321760491236276)
XLA Ops:
  15.6 5.4 copy.212
  21.0 6.9 copy.206
  28.1 316.5 %all-gather = f32[128,1,32]{2,1,0:T(1,128)S(1)} all-gather(f32[1,1,32]{2,1,0:T(1,128)S(1)} %reshape.135), channel_id=1, replica_groups=mesh['prow'=8,'pcol'=8,'orb'=2] {'prow','pcol','orb'}, dimensions={0}, use_global_device_ids=true | all-gather | bytes 16512 | tf_op jit(solution)/shard_map/all_gather | solution.py:47
  346.9 8.1 multiply_bitcast_fusion
  354.9 7.9 reshape.94
  362.8 7.9 reshape.100
  370.9 308.4 %all-gather.1 = f32[128,1,32]{2,1,0:T(1,128)S(1)} all-gather(f32[1,1,32]{2,1,0:T(1,128)S(1)} %reshape.137), channel_id=1, replica_groups=mesh['prow'=8,'pcol'=8,'orb'=2] {'prow','pcol','orb'}, dimensions={0}, use_global_device_ids=true | all-gather | bytes 16512 | tf_op jit(solution)/shard_map/all_gather | solution.py:48
  680.0 4.1 gather_fusion.2
  684.5 310.6 %all-gather.3 = f32[128,1,32]{2,1,0:T(1,128)S(1)} all-gather(f32[1,1,32]{2,1,0:T(1,128)S(1)} %reshape.141), channel_id=1, replica_groups=mesh['prow'=8,'pcol'=8,'orb'=2] {'prow','pcol','orb'}, dimensions={0}, use_global_device_ids=true | all-gather | bytes 16512 | tf_op jit(solution)/shard_map/all_gather | solution.py:110
  995.8 4.2 gather_fusion.1
  1000.3 308.6 %all-gather.2 = f32[128,1,32]{2,1,0:T(1,128)S(1)} all-gather(f32[1,1,32]{2,1,0:T(1,128)S(1)} %reshape.139), channel_id=1, replica_groups=mesh['prow'=8,'pcol'=8,'orb'=2] {'prow','pcol','orb'}, dimensions={0}, use_global_device_ids=true | all-gather | bytes 16512 | tf_op jit(solution)/shard_map/all_gather | solution.py:109
  1319.5 5.6 copy.171
  1325.1 5.6 copy.169
  1330.7 6.9 fusion
  1337.6 4.4 fusion.26
  1345.1 7.3 fusion.2
  1352.4 4.4 fusion.23
  1359.9 11.8 fusion.8
  1371.7 13.6 fusion.34
  1387.5 3.0 fusion.15
  1393.4 2.6 reshape.165
  1396.0 11.2 fusion.9
  1407.3 11.2 fusion.31
  1420.7 2.9 fusion.19
  (115 shorter events, 39.9 us)
Async XLA Ops:
  7.2 3.2 copy-start.7
  7.2 1312.3 %all-gather.13.cloned.1.call-start = ((), (), s32[]{:S(2)}) async-start(), calls=%async_computation.2 | async-start | bytes 4718592 | tf_op jit(solution)/shard_map/all_gather | solution.py:60
  10.3 1314.8 %all-gather.9.cloned.1.call-start = ((), (), s32[]{:S(2)}) async-start(), calls=%async_computation | async-start | bytes 4718592 | tf_op jit(solution)/shard_map/all_gather | solution.py:61
  10.7 2.9 copy-start.4
  12.3 1347.5 %all-gather.15.cloned.1.call-start = ((), (), s32[]{:S(2)}) async-start(), calls=%async_computation.3 | async-start | bytes 8912896 | tf_op jit(solution)/shard_map/all_gather | solution.py:71
  13.0 1358.6 %all-gather.11.cloned.1.call-start = ((), (), s32[]{:S(2)}) async-start(), calls=%async_computation.1 | async-start | bytes 8912896 | tf_op jit(solution)/shard_map/all_gather | solution.py:70
  21.0 6.9 copy-start.11
  21.0 324.2 %copy-start.10 = (f32[64,64]{1,0:T(8,128)S(1)}, f32[64,64]{1,0:T(8,128)}, u32[]{:S(2)}) copy-start(f32[64,64]{1,0:T(8,128)} %param.11) | copy-start | bytes 49156
  21.0 324.3 %copy-start.9 = (f32[64,64]{1,0:T(8,128)S(1)}, f32[64,64]{1,0:T(8,128)}, u32[]{:S(2)}) copy-start(f32[64,64]{1,0:T(8,128)} %param.12) | copy-start | bytes 49156
  21.0 324.4 %copy-start.8 = (f32[64,64]{1,0:T(8,128)S(1)}, f32[64,64]{1,0:T(8,128)}, u32[]{:S(2)}) copy-start(f32[64,64]{1,0:T(8,128)} %param.13) | copy-start | bytes 49156
  362.8 7.9 copy-start.12
  1330.7 6.9 copy-start
  1345.1 7.3 copy-start.1
  1387.5 3.0 copy-start.5
  1396.0 11.2 copy-start.2
  1396.0 11.2 copy-start.3
  1396.0 11.3 copy-start.6
Sparse Core Ops, SparseCore 0:
  10.4 34.7 all-gather.12
  47.5 32.1 all-gather.8
  81.9 177.6 all-gather.14
  261.7 183.1 all-gather.10
where the time goes:
time: 1440 us; the launch traced here: 1430 us
  blocking collectives  1240 us (86%)
  matrix products  89.3 us (6%)
  local copies, waits for them, and re-layouts  76.1 us (5%)
  between operations  14.5 us (1%)
    all_gather x1, blocking collectives, on_device(): lax.all_gather(flat_parts[0], ('prow', 'pcol', 'orb'), axis=0, tiled=True)  317 us
    all_gather x1, blocking collectives, on_device(): lax.all_gather(collide_parts[1], ('prow', 'pcol', 'orb'), axis=0, tiled=T...  311 us
    all_gather x1, blocking collectives, on_device(): lax.all_gather(collide_parts[0], ('prow', 'pcol', 'orb'), axis=0, tiled=T...  309 us
    all_gather x1, blocking collectives, on_device(): lax.all_gather(flat_parts[1], ('prow', 'pcol', 'orb'), axis=0, tiled=True)  308 us
  transfers between devices with their start and end apart: 4, of which 0 were waited for; matrix products, arithmetic and copies ran while one was open for 8% of the time, Pallas kernels for 0%

commit v1 on v0

v1 whole, which is shorter than its diff:
```python
import functools

import jax
import jax.numpy as jnp
from jax import lax
from jax.experimental import pallas as pl
from jax.experimental.pallas import tpu as pltpu
from jax.sharding import PartitionSpec as P

HIGH = lax.Precision.HIGHEST
MESH = pl.DeviceIdType.MESH
F32 = jnp.float32
BF16 = jnp.bfloat16

ORB = 64
ROWS = 8
COLS = 4


def dot(a, b):
    return jnp.dot(a, b, precision=HIGH, preferred_element_type=F32)


def mxu(a, b):
    return jnp.dot(a, b, preferred_element_type=F32)


def iota(shape, dim):
    return lax.broadcasted_iota(jnp.int32, shape, dim)


def split(value):
    high = value.astype(BF16)
    return high, (value - high.astype(F32)).astype(BF16)


def half_swap(first, second, lower):
    return (
        jnp.where(lower, first, pltpu.roll(second, 64, 1)),
        jnp.where(lower, pltpu.roll(first, 64, 1), second),
    )


def kernel(
    g2r,
    g2i,
    g1r,
    g1i,
    hop_r,
    hop_i,
    coup,
    hop_r_s,
    hop_i_s,
    out_r,
    out_i,
    d1_r,
    d1_i,
    right,
    left,
    left_send,
    stack,
    lcat,
    part,
    part_in,
    small_y,
    small_x,
    small_z,
    field_rows,
    kron,
    wide,
    send,
    recv,
):
    prow, pcol, orb = (lax.axis_index(n) for n in ("prow", "pcol", "orb"))
    z, c = prow // 2, prow % 2
    x = pcol % 4
    y = (pcol // 4) * 2 + orb
    rb = prow

    def at(dx=0, dy=0, dz=0, dc=0):
        xx, yy, zz, cc = (x + dx) % 4, (y + dy) % 4, (z + dz) % 4, (c + dc) % 2
        return (zz * 2 + cc, (yy // 2) * 4 + xx, yy % 2)

    def col_block(xx, yy):
        return (yy // 2) * 8 + xx * 2 + yy % 2

    cb = col_block(x, y)
    ya = y + 1 - 2 * orb
    yb = (y + 3 + 2 * orb) % 4
    dev_a = (prow, (ya // 2) * 4 + x, ya % 2)
    dev_b = (prow, (yb // 2) * 4 + x, yb % 2)

    partners = [
        at(dc=1),
        at(dx=1),
        at(dx=3),
        at(dx=2),
        at(dy=1),
        at(dy=3),
        at(dy=2),
        at(dz=1),
        at(dz=3),
        at(dz=2),
    ]
    barrier = pltpu.get_barrier_semaphore()
    for device in partners:
        pl.semaphore_signal(barrier, inc=1, device_id=device, device_id_type=MESH)

    sent = []

    def push(src, dst, device):
        n = len(sent)
        copy = pltpu.make_async_remote_copy(
            src_ref=src,
            dst_ref=dst,
            send_sem=send.at[n],
            recv_sem=recv.at[n],
            device_id=device,
            device_id_type=MESH,
        )
        copy.start()
        sent.append(copy)
        return copy

    lower = iota((64, 128), 1) < 64
    for comp, g in ((0, g2r), (1, g2i)):
        for kt in range(2):
            lanes = slice(kt * 128, kt * 128 + 128)
            for ip in range(4):
                even, odd = half_swap(
                    g[ip * 128 : ip * 128 + 64, lanes],
                    g[ip * 128 + 64 : ip * 128 + 128, lanes],
                    lower,
                )
                to = slice(ip * 128, ip * 128 + 128)
                right[0, 2 * kt, comp, :, to] = even
                right[0, 2 * kt + 1, comp, :, to] = odd
    mine = pl.ds(pl.multiple_of(orb * 256, 256), 256)
    other = pl.ds(pl.multiple_of((1 - orb) * 256, 256), 256)
    for comp in range(2):
        for k in range(4):
            left[rb, 0, comp, k * 64 : k * 64 + 64, :] = right[0, k, comp, :, mine]
            left_send[k // 2, comp, (k % 2) * 64 : (k % 2) * 64 + 64, :] = right[
                0, k, comp, :, other
            ]

    same = iota((64, 256), 0) == iota((64, 256), 1) % 64
    repeat = same.astype(F32)
    wide[...] = dot(coup[...], repeat)
    diag_r = jnp.concatenate(
        [jnp.sum(jnp.where(same, g2r[i * 64 : i * 64 + 64, :], 0.0), 0, keepdims=True) for i in range(ROWS)], 0
    )
    diag_i = jnp.concatenate(
        [jnp.sum(jnp.where(same, g2i[i * 64 : i * 64 + 64, :], 0.0), 0, keepdims=True) for i in range(ROWS)], 0
    )
    weight = wide[pl.ds(pl.multiple_of(rb * ROWS, ROWS), ROWS), :]
    place = iota((256, 128), 1) - COLS * cb
    group = iota((256, 128), 0) // 64
    to_re = (place == group).astype(F32)
    to_im = (place == group + 64).astype(F32)
    small_y[0, 8:16, :] = dot(weight * diag_i, to_re) - dot(weight * diag_r, to_im)
    spot = iota((8, 128), 1) - COLS * cb
    tile = jnp.zeros((8, 128), F32)
    for q in range(COLS):
        tile = tile + jnp.where(spot == q, g1r[:, q : q + 1], 0.0)
        tile = tile + jnp.where(spot == q + 64, g1i[:, q : q + 1], 0.0)
    small_y[0, 0:8, :] = tile

    pl.semaphore_wait(barrier, len(partners))

    tiny_y = [
        push(small_y.at[0], small_y.at[n], at(dy=d)) for n, d in ((1, 1), (2, 3), (3, 2))
    ]
    pre = [
        push(left_send.at[0], left.at[rb, 1, :, 0:128, :], dev_a),
        push(left_send.at[1], left.at[rb, 1, :, 128:256, :], dev_b),
    ]
    z_first = {}
    for d, name in ((1, "m"), (3, "p")):
        z_first[name, 0] = push(left.at[rb, 0], left.at[rb, 0], at(dz=d))
    got = {}
    for a in range(4):
        got[1, a] = push(right.at[0, a], right.at[1, a], at(dy=2))
        got[2, a] = push(right.at[0, a], right.at[2, a], at(dx=1))
        got[4, a] = push(right.at[0, a], right.at[4, a], at(dx=3))
    sib = [push(left.at[rb, 0], left.at[rb, 0], at(dc=1))]

    eye = (iota((64, 64), 0) == iota((64, 64), 1)).astype(F32)
    hr, hi = hop_r[...], hop_i[...]
    off_r = 0.5 * (hr + hr.T) * (1.0 - eye)
    off_i = 0.5 * (hi - hi.T)
    choose = (iota((64, 512), 0) == rb * ROWS + iota((64, 512), 1) // 64).astype(F32)
    field_rows[0] = dot(off_r, choose)
    field_rows[1] = -dot(off_i, choose)
    block_diag = iota((256, 256), 0) // 64 == iota((256, 256), 1) // 64
    tall = (iota((256, 64), 0) % 64 == iota((256, 64), 1)).astype(F32)
    kron[0] = jnp.where(block_diag, dot(tall, dot(off_r, repeat)), 0.0)
    kron[1] = jnp.where(block_diag, dot(tall, dot(off_i, repeat)), 0.0)
    coup_t = coup[...].T

    def where_is(slot):
        dx = (0, 3, 1, 2)[slot // 2]
        return (x + dx) % 4, (y + 2 * (slot % 2)) % 4

    def prepare(slot):
        base = col_block(*where_is(slot)) * COLS
        match = iota((64, 512), 0) == iota((64, 512), 1) % 64
        for a in range(4):
            v = jnp.sum(
                jnp.where(iota((64, 64), 1) == base + a, coup_t, 0.0), 1, keepdims=True
            )
            for comp in range(2):
                value = v * right[slot, a, comp] + jnp.where(
                    match, field_rows[comp, pl.ds(base + a, 1), :], 0.0
                )
                high, low = split(value)
                at_row = comp * 256 + a * 64
                stack[slot, at_row : at_row + 64, :] = high
                stack[slot, 512 + at_row : 512 + at_row + 64, :] = low

    def mix(slot):
        base = col_block(*where_is(slot)) * COLS
        starts = (cb * COLS, col_block(x, ya) * COLS, col_block(x, yb) * COLS)
        scale = {}
        for kk in range(8):
            k = starts[0] + kk if kk < 4 else starts[1 if kk < 6 else 2] + kk - 4
            for a in range(4):
                if slot == 0 and a == kk:
                    continue
                scale[kk, a] = (
                    0.5 * (hop_r_s[base + a, k] + hop_r_s[k, base + a]),
                    0.5 * (hop_i_s[base + a, k] - hop_i_s[k, base + a]),
                )

        @pl.loop(0, 16)
        def _(step):
            strip, half = step // 2, step % 2
            lanes = pl.ds(pl.multiple_of(half * 256, 256), 256)
            rows = pl.ds(pl.multiple_of(strip * 8, 8), 8)
            tr = [right[slot, a, 0, rows, lanes] for a in range(4)]
            ti = [right[slot, a, 1, rows, lanes] for a in range(4)]
            for kk in range(8):
                to = pl.ds(pl.multiple_of((kk % 2) * 64 + strip * 8, 8), 8)
                acc_r = acc_i = None
                for a in range(4):
                    if (kk, a) not in scale:
                        continue
                    sr, si = scale[kk, a]
                    vr = si * ti[a] - sr * tr[a]
                    vi = sr * ti[a] + si * tr[a]
                    acc_r = vr if acc_r is None else acc_r + vr
                    acc_i = -vi if acc_i is None else acc_i - vi
                if slot == 0:
                    part[kk // 2, 0, to, lanes] = acc_r
                    part[kk // 2, 1, to, lanes] = acc_i
                else:
                    part[kk // 2, 0, to, lanes] += acc_r
                    part[kk // 2, 1, to, lanes] += acc_i

    def multiply(slot, half):
        xx, yy = where_is(slot)
        which = (yy // 2) * 4 + xx
        lr_h, lr_l = split(left[which, half, 0])
        li_h, li_l = split(left[which, half, 1])
        for n, (re, im) in enumerate(((lr_h, li_h), (lr_l, li_l))):
            lcat[0, :, n * 512 : n * 512 + 256] = re
            lcat[0, :, n * 512 + 256 : n * 512 + 512] = -im
            lcat[1, :, n * 512 : n * 512 + 256] = im
            lcat[1, :, n * 512 + 256 : n * 512 + 512] = re

        @pl.loop(0, 4)
        def _(step):
            comp, side = step // 2, step % 2
            lanes = pl.ds(pl.multiple_of(side * 256, 256), 256)
            high = lcat[comp, :, 0:512]
            value = (
                mxu(high, stack[slot, 0:512, lanes])
                + mxu(high, stack[slot, 512:1024, lanes])
                + mxu(lcat[comp, :, 512:1024], stack[slot, 0:512, lanes])
            )
            part[2 * half, comp, :, lanes] += value[0:128]
            part[2 * half + 1, comp, :, lanes] += value[128:256]

    prepare(0)
    mix(0)

    for copy in tiny_y:
        copy.wait_recv()
    small_x[0] = small_y[0] + small_y[1] + small_y[2] + small_y[3]
    tiny_x = [
        push(small_x.at[0], small_x.at[n], at(dx=d)) for n, d in ((1, 1), (2, 3), (3, 2))
    ]

    for copy in pre:
        copy.wait_recv()
    for d, name in ((1, "m"), (3, "p")):
        z_first[name, 1] = push(left.at[rb, 1], left.at[rb, 1], at(dz=d))
    sib.append(push(left.at[rb, 1], left.at[rb, 1], at(dc=1)))

    for half in range(2):
        rows = slice(half * 256, half * 256 + 256)
        gr, gi = g2r[rows, :], g2i[rows, :]
        kr, ki = kron[0], kron[1]
        out_r[rows, :] = dot(kr, gi) + dot(ki, gr) - dot(gr, ki) - dot(gi, kr)
        out_i[rows, :] = dot(ki, gi) - dot(kr, gr) + dot(gr, kr) - dot(gi, ki)

    for copy in tiny_x:
        copy.wait_recv()
    small_z[c, z] = small_x[0] + small_x[1] + small_x[2] + small_x[3]
    tiny_z = [
        push(small_z.at[c, z], small_z.at[c, z], at(dz=d)) for d in (1, 3, 2)
    ]

    rb_m = ((z + 3) % 4) * 2 + c
    rb_p = ((z + 1) % 4) * 2 + c
    rb_2 = ((z + 2) % 4) * 2 + c
    z_second = {}

    def pass_on(p):
        z_first["m", p].wait_recv()
        z_second[0, p] = push(left.at[rb_m, p, 0], left.at[rb_m, p, 0], at(dz=1))
        sib.append(push(left.at[rb_m, p], left.at[rb_m, p], at(dc=1)))
        z_first["p", p].wait_recv()
        z_second[1, p] = push(left.at[rb_p, p, 1], left.at[rb_p, p, 1], at(dz=3))
        sib.append(push(left.at[rb_p, p], left.at[rb_p, p], at(dc=1)))

    pass_on(0)

    for copy in tiny_z:
        copy.wait_recv()
    tiny_c = push(small_z.at[c], small_z.at[c], at(dc=1))

    for a in range(3):
        got[1, a].wait_recv()
        got[3, a] = push(right.at[1, a], right.at[3, a], at(dx=1))
        got[5, a] = push(right.at[1, a], right.at[5, a], at(dx=3))
    got[1, 3].wait_recv()
    prepare(1)
    mix(1)
    tiny_c.wait_recv()

    rows_z = [(r // 2, r % 2) for r in range(8)]
    one = jnp.concatenate([small_z[cc, zz, 0:8, :] for zz, cc in rows_z], 0)
    coll = jnp.concatenate([small_z[cc, zz, 8:16, :] for zz, cc in rows_z], 0)
    gr, gi = one[:, 0:64], one[:, 64:128]
    cr, ci = coll[:, 0:64], coll[:, 64:128]
    density = jnp.sum(gr * eye, 0, keepdims=True)
    hartree_col = jnp.sum(coup[...] * density, 1, keepdims=True)
    diag_col = hartree_col + jnp.sum(hr * eye, 1, keepdims=True)
    diag_row = jnp.sum(diag_col * eye, 0, keepdims=True)
    fr = off_r + diag_col * eye
    fi = off_i
    comm_r = dot(fr, gr) - dot(fi, gi) - dot(gr, fr) + dot(gi, fi)
    comm_i = dot(fr, gi) + dot(fi, gr) - dot(gr, fi) - dot(gi, fr)
    d1_r[...] = comm_i + cr + cr.T
    d1_i[...] = ci - ci.T - comm_r

    from_cols = jnp.zeros((1, 256), F32)
    lane_group = iota((1, 256), 1) // 64
    row64 = iota((64, 64), 0)
    table = coup[...] + diag_col + diag_row
    table_wide = dot(table, repeat)
    row_wide = iota((64, 256), 0)
    for k in range(COLS):
        picked = jnp.sum(
            jnp.where(row_wide == cb * COLS + k, table_wide, 0.0), 0, keepdims=True
        )
        from_cols = jnp.where(lane_group == k, picked, from_cols)
    table_t = coup_t + diag_col + diag_row
    for i in range(ROWS):
        from_rows = jnp.sum(
            jnp.where(iota((64, 64), 1) == rb * ROWS + i, table_t, 0.0), 1, keepdims=True
        )
        rows = slice(i * 64, i * 64 + 64)
        factor = from_rows - from_cols
        out_r[rows, :] += factor * g2i[rows, :]
        out_i[rows, :] -= factor * g2r[rows, :]

    for a in range(4):
        got[2, a].wait_recv()
        got[4, a].wait_recv()
        if a < 3:
            got[6, a] = push(right.at[2, a], right.at[6, a], at(dx=1))
        else:
            last = [
                push(right.at[2, 3, 0], right.at[6, 3, 0], at(dx=1)),
                push(right.at[4, 3, 1], right.at[6, 3, 1], at(dx=3)),
            ]
            got[3, 3] = push(right.at[2, 3], right.at[3, 3], at(dy=2))
            got[5, 3] = push(right.at[4, 3], right.at[5, 3], at(dy=2))
    pass_on(1)
    prepare(2)
    mix(2)
    prepare(4)
    mix(4)
    z_second[0, 0].wait_recv()
    z_second[1, 0].wait_recv()
    sib.append(push(left.at[rb_2, 0], left.at[rb_2, 0], at(dc=1)))
    for copy in last:
        copy.wait_recv()
    got[7, 3] = push(right.at[6, 3], right.at[7, 3], at(dy=2))
    for a in range(3):
        got[5, a].wait_recv()
        got[7, a] = push(right.at[5, a], right.at[7, a], at(dx=3))
    z_second[0, 1].wait_recv()
    z_second[1, 1].wait_recv()
    sib.append(push(left.at[rb_2, 1], left.at[rb_2, 1], at(dc=1)))
    got[5, 3].wait_recv()
    prepare(5)
    mix(5)
    for a in range(4):
        got[3, a].wait_recv()
    prepare(3)
    mix(3)
    for copy in sib:
        copy.wait_recv()
    for slot in (0, 1, 2, 4, 5, 3):
        multiply(slot, 0)
        multiply(slot, 1)
    for a in range(3):
        got[6, a].wait_recv()
    prepare(6)
    mix(6)
    multiply(6, 0)
    multiply(6, 1)
    for a in range(4):
        got[7, a].wait_recv()
    prepare(7)
    mix(7)
    multiply(7, 1)
    sums = [
        push(part.at[2], part_in.at[0], dev_a),
        push(part.at[3], part_in.at[1], dev_b),
    ]
    multiply(7, 0)

    for g in range(2):
        sums[g].wait_recv()
        lanes = slice(g * 128, g * 128 + 128)
        for comp in range(2):
            for ip in range(4):
                cut = slice(ip * 128, ip * 128 + 128)
                even, odd = half_swap(
                    part[g, comp, 0:64, cut] + part_in[g, comp, 0:64, cut],
                    part[g, comp, 64:128, cut] + part_in[g, comp, 64:128, cut],
                    lower,
                )
                lo = slice(ip * 128, ip * 128 + 64)
                hi_rows = slice(ip * 128 + 64, ip * 128 + 128)
                if comp == 0:
                    out_i[lo, lanes] -= even
                    out_i[hi_rows, lanes] -= odd
                else:
                    out_r[lo, lanes] += even
                    out_r[hi_rows, lanes] += odd
    for copy in sent:
        copy.wait_send()


def on_device(g2_re, g2_im, g1_re, g1_im, hop_re, hop_im, coupling):
    vmem = pl.BlockSpec(memory_space=pltpu.VMEM)
    smem = pl.BlockSpec(memory_space=pltpu.SMEM)
    count = 72
    return pl.pallas_call(
        kernel,
        out_shape=(
            jax.ShapeDtypeStruct((512, 256), F32),
            jax.ShapeDtypeStruct((512, 256), F32),
            jax.ShapeDtypeStruct((64, 64), F32),
            jax.ShapeDtypeStruct((64, 64), F32),
        ),
        in_specs=[vmem] * 7 + [smem] * 2,
        out_specs=(vmem,) * 4,
        scratch_shapes=[
            pltpu.VMEM((8, 4, 2, 64, 512), F32),
            pltpu.VMEM((8, 2, 2, 256, 256), F32),
            pltpu.VMEM((2, 2, 128, 256), F32),
            pltpu.VMEM((8, 1024, 512), BF16),
            pltpu.VMEM((2, 256, 1024), BF16),
            pltpu.VMEM((4, 2, 128, 512), F32),
            pltpu.VMEM((2, 2, 128, 512), F32),
            pltpu.VMEM((4, 16, 128), F32),
            pltpu.VMEM((4, 16, 128), F32),
            pltpu.VMEM((2, 4, 16, 128), F32),
            pltpu.VMEM((2, 64, 512), F32),
            pltpu.VMEM((2, 256, 256), F32),
            pltpu.VMEM((64, 256), F32),
            pltpu.SemaphoreType.DMA((count,)),
            pltpu.SemaphoreType.DMA((count,)),
        ],
        compiler_params=pltpu.CompilerParams(
            collective_id=0, has_side_effects=True, vmem_limit_bytes=56 * 2**20
        ),
    )(g2_re, g2_im, g1_re, g1_im, hop_re, hop_im, coupling, hop_re, hop_im)


def solution(mesh):
    pairs = P("prow", ("pcol", "orb"))
    return jax.shard_map(
        on_device,
        mesh=mesh,
        in_specs=(pairs, pairs, pairs, pairs, P(), P(), P()),
        out_specs=(pairs, pairs, P(), P()),
        check_vma=False,
    )
```

time: 1440 us -> 129 us (0.09)
  blocking collectives: 1240 us -> 0 us
  Pallas kernels: 0 us -> 122 us
  matrix products: 89.3 us -> 0 us
  local copies, waits for them, and re-layouts: 76.1 us -> 6.14 us
    all_gather x4 -> x0, blocking collectives: 1240 us -> none  [the longest x1 317 us: on_device(): lax.all_gather(flat_parts[0], ('prow', 'pcol', 'orb'), axis=0, tiled=True)]
    pallas_call x0 -> x1, Pallas kernels: none -> 122 us  [on_device(): pl.pallas_call(kernel, out_shape=(jax.ShapeDtypeStruct((512, 256), F32),...]
    dot_general x27 -> x0, matrix products: 89.3 us -> none  [the longest x1 13.6 us: on_device(): jnp.dot(piece_re, right_re, precision=HIGH)]
    reshape x24 -> x0, local copies, waits for them, and re-layouts: 42.4 us -> none  [the longest x8 19.2 us: to_hole(): shaped = block.reshape(row_orbs, orbits, col_orbs, orbits)]
  transfers between devices with their start and end apart: 4 -> 0, of which waited for: 0 -> 0; matrix products, arithmetic and copies ran while one was open for 8% -> 0% of each run, Pallas kernels for 0% -> 0%
where the time goes in v1:
time: 129 us; the launch traced here: 128 us
  Pallas kernels  122 us (95%)
  local copies, waits for them, and re-layouts  6.14 us (5%)
    pallas_call x1, Pallas kernels, on_device(): pl.pallas_call(kernel, out_shape=(jax.ShapeDtypeStruct((512, 256), F32),...  122 us
    unnamed x14, local copies, waits for them, and re-layouts  6.14 us

profile of v1, /device:TPU:0, one launch (start us, length us, event | category | flops | bytes accessed | tf_op | source)
XLA Modules:
  0.0 128.4 jit_solution(725263782340228165)
XLA Ops:
  0.6 0.0 copy-start.3
  0.6 1.4 %copy.11.g1r = f32[8,4]{1,0:T(8,128)} copy(f32[8,4]{0,1:T(4,128)} %param.9) | data formatting | bytes 256 | tf_op args[2]
  2.0 0.0 copy-done.3
  2.0 0.7 copy.12.g1i
  2.7 121.6 %shard_map.102 = (f32[512,256]{1,0:T(8,128)}, f32[512,256]{1,0:T(8,128)}, f32[64,64]{1,0:T(8,128)}, f32[64,64]{1,0:T(8,128)}) custom-call(f32[512,256]{1,0:T(8,128)} %g2r.1, f32[512,256]{1,0:T(8,128)} %g2i.1, f32[8,4]{1,0:T(8,128)} %copy.11.g1r, f32[8,4]{1,0:T(8,128)} %copy.12.g1i, f32[64,64]{1,0:T(8,128)} %hop_r_s.1, f32[64,64]{1,0:T(8,128)} %hop_i_s.1, ...), custom_call_target="tpu_custom_call" | custom-call | tf_op jit(solution)/shard_map/pallas_call | solution.py:464
  124.3 0.0 copy-start
  124.3 1.9 %copy.17 = f32[512,256]{1,0:T(8,128)} copy(f32[512,256]{1,0:T(8,128)} %get-tuple-element.8) | data formatting | bytes 1048576
  126.2 0.0 copy-done
  126.2 0.0 copy-start.2
  126.2 0.8 copy.18
  127.0 0.0 copy-done.2
  127.0 0.0 copy-start.1
  127.0 0.6 copy.19
  127.6 0.2 copy-done.1
  127.8 0.6 copy.20
Async XLA Ops:
  0.6 1.4 %copy-start.3 = (f32[8,4]{0,1:T(4,128)S(1)}, f32[8,4]{0,1:T(4,128)}, u32[]{:S(2)}) copy-start(f32[8,4]{0,1:T(4,128)} %param.10) | copy-start | bytes 388
  124.3 1.9 %copy-start = (f32[512,256]{1,0:T(8,128)S(1)}, f32[512,256]{1,0:T(8,128)}, u32[]{:S(2)}) copy-start(f32[512,256]{1,0:T(8,128)} %get-tuple-element.9) | copy-start | bytes 1572868
  126.2 0.8 copy-start.2
  127.0 0.8 copy-start.1

commit v2 on v1

v2 whole, which is shorter than its diff:
```python
import functools

import jax
import jax.numpy as jnp
from jax import lax
from jax.experimental import pallas as pl
from jax.experimental.pallas import tpu as pltpu
from jax.sharding import PartitionSpec as P

HIGH = lax.Precision.HIGHEST
MESH = pl.DeviceIdType.MESH
F32 = jnp.float32
BF16 = jnp.bfloat16

ORB = 64
ROWS = 8
COLS = 4


def dot(a, b):
    return jnp.dot(a, b, precision=HIGH, preferred_element_type=F32)


def mxu(a, b):
    return jnp.dot(a, b, preferred_element_type=F32)


def iota(shape, dim):
    return lax.broadcasted_iota(jnp.int32, shape, dim)


def split(value):
    high = value.astype(BF16)
    return high, (value - high.astype(F32)).astype(BF16)


def half_swap(first, second, lower):
    return (
        jnp.where(lower, first, pltpu.roll(second, 64, 1)),
        jnp.where(lower, pltpu.roll(first, 64, 1), second),
    )


def kernel(
    g2r,
    g2i,
    g1r,
    g1i,
    hop_r,
    hop_i,
    coup,
    hop_r_s,
    hop_i_s,
    out_r,
    out_i,
    d1_r,
    d1_i,
    right,
    left,
    left_send,
    stack,
    lsplit,
    part,
    part_in,
    small_y,
    small_x,
    small_z,
    field_rows,
    kron,
    wide,
    send,
    recv,
):
    prow, pcol, orb = (lax.axis_index(n) for n in ("prow", "pcol", "orb"))
    z, c = prow // 2, prow % 2
    x = pcol % 4
    y = (pcol // 4) * 2 + orb
    rb = prow

    def at(dx=0, dy=0, dz=0, dc=0):
        xx, yy, zz, cc = (x + dx) % 4, (y + dy) % 4, (z + dz) % 4, (c + dc) % 2
        return (zz * 2 + cc, (yy // 2) * 4 + xx, yy % 2)

    def col_block(xx, yy):
        return (yy // 2) * 8 + xx * 2 + yy % 2

    cb = col_block(x, y)
    ya = y + 1 - 2 * orb
    yb = (y + 3 + 2 * orb) % 4
    dev_a = (prow, (ya // 2) * 4 + x, ya % 2)
    dev_b = (prow, (yb // 2) * 4 + x, yb % 2)

    partners = [
        at(dc=1),
        at(dx=1),
        at(dx=3),
        at(dx=2),
        at(dy=1),
        at(dy=3),
        at(dy=2),
        at(dz=1),
        at(dz=3),
        at(dz=2),
    ]
    barrier = pltpu.get_barrier_semaphore()
    for device in partners:
        pl.semaphore_signal(barrier, inc=1, device_id=device, device_id_type=MESH)

    sent = []

    def push(src, dst, device):
        n = len(sent)
        copy = pltpu.make_async_remote_copy(
            src_ref=src,
            dst_ref=dst,
            send_sem=send.at[n],
            recv_sem=recv.at[n],
            device_id=device,
            device_id_type=MESH,
        )
        copy.start()
        sent.append(copy)
        return copy

    lower = iota((64, 128), 1) < 64
    for ch in range(2):
        for comp, g in ((0, g2r), (1, g2i)):
            for kt in range(2):
                lanes = slice(kt * 128, kt * 128 + 128)
                for ip in range(2):
                    top = ch * 256 + ip * 128
                    even, odd = half_swap(
                        g[top : top + 64, lanes], g[top + 64 : top + 128, lanes], lower
                    )
                    to = slice(ip * 128, ip * 128 + 128)
                    right[0, ch, 4 * kt + comp, :, to] = even
                    right[0, ch, 4 * kt + 2 + comp, :, to] = odd
    for comp in range(2):
        for k in range(4):
            left[rb, 0, comp, k * 64 : k * 64 + 64, :] = right[0, orb, 2 * k + comp]
            left_send[k // 2, comp, (k % 2) * 64 : (k % 2) * 64 + 64, :] = right[
                0, 1 - orb, 2 * k + comp
            ]

    pl.semaphore_wait(barrier, len(partners))

    got = {}

    def go(to, start, ch, first, last, device):
        cut = pl.ds(first, last - first)
        got[to, ch, first] = push(right.at[start, ch, cut], right.at[to, ch, cut], device)

    def arrived(slot, ch, *firsts):
        for first in firsts:
            got[slot, ch, first].wait_recv()

    def own_y(ch, first, last):
        go(1, 0, ch, first, last, at(dy=2))

    def own_x(ch, first, last):
        go(6, 0, ch, first, last, at(dx=1))
        go(2, 0, ch, first, last, at(dx=3))

    own_y(0, 0, 3)
    own_x(0, 6, 8)
    own_x(0, 0, 6)
    pre = [
        push(left_send.at[0], left.at[rb, 1, :, 0:128, :], dev_a),
        push(left_send.at[1], left.at[rb, 1, :, 128:256, :], dev_b),
    ]
    z_first = {}
    for d, name in ((1, "m"), (3, "p")):
        z_first[name, 0] = push(left.at[rb, 0], left.at[rb, 0], at(dz=d))
    own_y(0, 3, 6)
    own_y(0, 6, 8)
    own_x(1, 6, 8)
    sib = {(0, 0): push(left.at[rb, 0], left.at[rb, 0], at(dc=1))}

    same = iota((64, 256), 0) == iota((64, 256), 1) % 64
    repeat = same.astype(F32)
    wide[...] = dot(coup[...], repeat)
    diag_r = jnp.concatenate(
        [jnp.sum(jnp.where(same, g2r[i * 64 : i * 64 + 64, :], 0.0), 0, keepdims=True) for i in range(ROWS)], 0
    )
    diag_i = jnp.concatenate(
        [jnp.sum(jnp.where(same, g2i[i * 64 : i * 64 + 64, :], 0.0), 0, keepdims=True) for i in range(ROWS)], 0
    )
    weight = wide[pl.ds(pl.multiple_of(rb * ROWS, ROWS), ROWS), :]
    place = iota((256, 128), 1) - COLS * cb
    group = iota((256, 128), 0) // 64
    to_re = (place == group).astype(F32)
    to_im = (place == group + 64).astype(F32)
    small_y[0, 8:16, :] = dot(weight * diag_i, to_re) - dot(weight * diag_r, to_im)
    spot = iota((8, 128), 1) - COLS * cb
    eye8 = iota((8, 8), 0) == iota((8, 8), 1)
    tile = jnp.zeros((8, 128), F32)
    for q in range(COLS):
        for lane, g1 in ((q, g1r), (q + 64, g1i)):
            column = jnp.sum(jnp.where(eye8, g1[q : q + 1, :], 0.0), 1, keepdims=True)
            tile = tile + jnp.where(spot == lane, column, 0.0)
    small_y[0, 0:8, :] = tile

    tiny_y = [
        push(small_y.at[0], small_y.at[n], at(dy=d)) for n, d in ((1, 1), (2, 3), (3, 2))
    ]

    eye = (iota((64, 64), 0) == iota((64, 64), 1)).astype(F32)
    hr, hi = hop_r[...], hop_i[...]
    off_r = 0.5 * (hr + hr.T) * (1.0 - eye)
    off_i = 0.5 * (hi - hi.T)
    choose = (iota((64, 512), 0) == rb * ROWS + iota((64, 512), 1) // 64).astype(F32)
    field_rows[0] = dot(off_r, choose)
    field_rows[1] = -dot(off_i, choose)
    block_diag = iota((256, 256), 0) // 64 == iota((256, 256), 1) // 64
    tall = (iota((256, 64), 0) % 64 == iota((256, 64), 1)).astype(F32)
    kron[0] = jnp.where(block_diag, dot(tall, dot(off_r, repeat)), 0.0)
    kron[1] = jnp.where(block_diag, dot(tall, dot(off_i, repeat)), 0.0)
    coup_t = coup[...].T

    def where_is(slot):
        return (x + slot // 2) % 4, (y + 2 * (slot % 2)) % 4

    for ch in range(2):
        for g in range(4):
            part[ch, g] = jnp.zeros((2, 128, 256), F32)

    def prepare(slot, ch):
        base = col_block(*where_is(slot)) * COLS
        match = iota((64, 256), 0) == iota((64, 256), 1) % 64
        for a in range(4):
            v = jnp.sum(
                jnp.where(iota((64, 64), 1) == base + a, coup_t, 0.0), 1, keepdims=True
            )
            for comp in range(2):
                value = v * right[slot, ch, 2 * a + comp] + jnp.where(
                    match,
                    field_rows[comp, pl.ds(base + a, 1), ch * 256 : ch * 256 + 256],
                    0.0,
                )
                for n, term in enumerate(split(value)):
                    row = n * 768 + (1 - comp) * 256 + a * 64
                    stack[slot, ch, row : row + 64, :] = term
                    if comp == 1:
                        stack[slot, ch, row + 512 : row + 576, :] = -term

    def mix(slot, ch):
        base = col_block(*where_is(slot)) * COLS
        starts = (cb * COLS, col_block(x, ya) * COLS, col_block(x, yb) * COLS)
        for kk in range(8):
            k = starts[0] + kk if kk < 4 else starts[1 if kk < 6 else 2] + kk - 4
            scale = []
            for a in range(4):
                sr = 0.5 * (hop_r_s[base + a, k] + hop_r_s[k, base + a])
                si = 0.5 * (hop_i_s[base + a, k] - hop_i_s[k, base + a])
                sr = jnp.where(k == base + a, 0.0, sr)
                scale.append((jnp.full((8, 256), sr, F32), jnp.full((8, 256), si, F32)))
            for strip in range(8):
                to = slice((kk % 2) * 64 + strip * 8, (kk % 2) * 64 + strip * 8 + 8)
                rows = slice(strip * 8, strip * 8 + 8)
                acc_r = part[ch, kk // 2, 0, to, :]
                acc_i = part[ch, kk // 2, 1, to, :]
                for a in range(4):
                    sr, si = scale[a]
                    tr = right[slot, ch, 2 * a, rows, :]
                    ti = right[slot, ch, 2 * a + 1, rows, :]
                    acc_r += si * ti - sr * tr
                    acc_i -= sr * ti + si * tr
                part[ch, kk // 2, 0, to, :] = acc_r
                part[ch, kk // 2, 1, to, :] = acc_i

    def enter(ch, first, count=1, stride=1):
        @pl.loop(0, count)
        def _(n):
            prepare(first + n * stride, ch)
            mix(first + n * stride, ch)

    def split_left(which, p):
        @pl.loop(0, 4)
        def _(step):
            rows = pl.ds(pl.multiple_of(step * 64, 64), 64)
            to = pl.ds(pl.multiple_of(p * 256 + step * 64, 64), 64)
            for comp in range(2):
                for n, term in enumerate(split(left[which, p, comp, rows, :])):
                    lane = n * 512 + comp * 256
                    lsplit[which, to, lane : lane + 256] = term

    def multiply(slot, ch, halves=(0, 1)):
        xx, yy = where_is(slot)
        which = (yy // 2) * 4 + xx
        rows = slice(halves[0] * 256, halves[-1] * 256 + 256)

        @pl.loop(0, 2)
        def _(comp):
            start = (1 - comp) * 256
            high = stack[slot, ch, pl.ds(pl.multiple_of(start, 256), 512), :]
            low = stack[slot, ch, pl.ds(pl.multiple_of(start + 768, 256), 512), :]
            value = (
                mxu(lsplit[which, rows, 0:512], high)
                + mxu(lsplit[which, rows, 0:512], low)
                + mxu(lsplit[which, rows, 512:1024], high)
            )
            for n in range(2 * len(halves)):
                part[ch, 2 * halves[0] + n, comp] += value[n * 128 : n * 128 + 128]

    def slot_of(zz, cc):
        return ((2 * (zz % 2) + cc - x + 4) % 4) * 2 + (zz // 2 + y // 2) % 2

    def along_x(ch, first):
        arrived(1, ch, first)
        go(7, 1, ch, first, first + 3, at(dx=1))
        go(3, 1, ch, first, first + 3, at(dx=3))

    def relay_few(ch):
        arrived(6, ch, 6)
        arrived(2, ch, 6)
        go(4, 6, ch, 6, 7, at(dx=1))
        go(4, 2, ch, 7, 8, at(dx=3))
        go(7, 6, ch, 6, 8, at(dy=2))
        go(3, 2, ch, 6, 8, at(dy=2))

    def relay(ch):
        arrived(6, ch, 0)
        go(4, 6, ch, 0, 6, at(dx=1))
        arrived(2, ch, 0)

    def relay_far(ch):
        arrived(4, ch, 6, 7)
        go(5, 4, ch, 6, 8, at(dy=2))

    def relay_last(ch, first):
        arrived(3, ch, first)
        go(5, 3, ch, first, first + 3, at(dx=3))

    rb_m = ((z + 3) % 4) * 2 + c
    rb_p = ((z + 1) % 4) * 2 + c
    rb_2 = ((z + 2) % 4) * 2 + c
    z_second = {}

    def pass_on(p):
        z_first["m", p].wait_recv()
        z_second[0, p] = push(left.at[rb_m, p, 0], left.at[rb_m, p, 0], at(dz=1))
        sib[3, p] = push(left.at[rb_m, p], left.at[rb_m, p], at(dc=1))
        z_first["p", p].wait_recv()
        z_second[1, p] = push(left.at[rb_p, p, 1], left.at[rb_p, p, 1], at(dz=3))
        sib[1, p] = push(left.at[rb_p, p], left.at[rb_p, p], at(dc=1))

    def pass_far(p):
        z_second[0, p].wait_recv()
        z_second[1, p].wait_recv()
        sib[2, p] = push(left.at[rb_2, p], left.at[rb_2, p], at(dc=1))
        split_left(rb_2, p)

    def from_sibling(dz):
        for p in range(2):
            sib[dz, p].wait_recv()
            split_left(((z + dz) % 4) * 2 + 1 - c, p)

    def by_left(dz):
        @pl.loop(0, 2)
        def _(cc):
            multiply(slot_of((z + dz) % 4, cc), 0)

    def times(first, count, stride, halves=(0, 1)):
        @pl.loop(0, count)
        def _(n):
            multiply(first + n * stride, 1, halves)

    sums = {}

    def send_sums(ch):
        sums[ch, 0] = push(part.at[ch, 2], part_in.at[ch, 0], dev_a)
        sums[ch, 1] = push(part.at[ch, 3], part_in.at[ch, 1], dev_b)

    along_x(0, 0)
    enter(0, 0)
    for copy in pre:
        copy.wait_recv()
    for d, name in ((1, "m"), (3, "p")):
        z_first[name, 1] = push(left.at[rb, 1], left.at[rb, 1], at(dz=d))
    sib[0, 1] = push(left.at[rb, 1], left.at[rb, 1], at(dc=1))
    relay_few(0)
    relay(0)
    along_x(0, 3)
    pass_on(0)
    own_y(1, 0, 3)
    own_y(1, 3, 6)
    own_y(1, 6, 8)
    for copy in tiny_y:
        copy.wait_recv()
    small_x[0] = small_y[0] + small_y[1] + small_y[2] + small_y[3]
    tiny_x = [
        push(small_x.at[0], small_x.at[n], at(dx=d)) for n, d in ((1, 1), (2, 3), (3, 2))
    ]
    split_left(rb, 0)
    split_left(rb, 1)
    split_left(rb_m, 0)
    split_left(rb_p, 0)
    arrived(1, 0, 6)
    enter(0, 1)
    relay_last(0, 0)
    enter(0, 2, 2, 4)
    relay_last(0, 3)
    own_x(1, 0, 6)
    relay_far(0)
    pass_on(1)
    for copy in tiny_x:
        copy.wait_recv()
    small_z[c, z] = small_x[0] + small_x[1] + small_x[2] + small_x[3]
    tiny_z = [
        push(small_z.at[c, z], small_z.at[c, z], at(dz=d)) for d in (1, 3, 2)
    ]
    along_x(1, 0)
    along_x(1, 3)
    split_left(rb_m, 1)
    split_left(rb_p, 1)
    arrived(3, 0, 6)
    arrived(7, 0, 0, 3, 6)
    enter(0, 3, 2, 4)
    from_sibling(0)
    enter(1, 0)
    arrived(1, 1, 6)
    enter(1, 1)
    pass_far(0)
    from_sibling(3)
    from_sibling(1)
    arrived(4, 0, 0)
    arrived(5, 0, 0, 3, 6)
    enter(0, 4, 2)
    by_left(0)
    by_left(3)
    by_left(1)
    for copy in tiny_z:
        copy.wait_recv()
    tiny_c = push(small_z.at[c], small_z.at[c], at(dc=1))
    pass_far(1)
    from_sibling(2)
    by_left(2)
    send_sums(0)
    relay_few(1)
    relay(1)
    enter(1, 2, 2, 4)
    times(0, 2, 1)
    relay_last(1, 0)
    times(2, 2, 4)
    relay_last(1, 3)
    relay_far(1)
    arrived(3, 1, 6)
    arrived(7, 1, 0, 3, 6)
    enter(1, 3, 2, 4)
    times(3, 2, 4)
    arrived(4, 1, 0)
    arrived(5, 1, 0, 3, 6)
    enter(1, 4, 2)
    times(4, 2, 1, (1,))
    send_sums(1)
    times(4, 2, 1, (0,))
    tiny_c.wait_recv()

    for half in range(2):
        rows = slice(half * 256, half * 256 + 256)
        gr, gi = g2r[rows, :], g2i[rows, :]
        kr, ki = kron[0], kron[1]
        out_r[rows, :] = dot(kr, gi) + dot(ki, gr) - dot(gr, ki) - dot(gi, kr)
        out_i[rows, :] = dot(ki, gi) - dot(kr, gr) + dot(gr, kr) - dot(gi, ki)

    rows_z = [(r // 2, r % 2) for r in range(8)]
    one = jnp.concatenate([small_z[cc, zz, 0:8, :] for zz, cc in rows_z], 0)
    coll = jnp.concatenate([small_z[cc, zz, 8:16, :] for zz, cc in rows_z], 0)
    gr, gi = one[:, 0:64], one[:, 64:128]
    cr, ci = coll[:, 0:64], coll[:, 64:128]
    density = jnp.sum(gr * eye, 0, keepdims=True)
    hartree_col = jnp.sum(coup[...] * density, 1, keepdims=True)
    diag_col = hartree_col + jnp.sum(hr * eye, 1, keepdims=True)
    diag_row = jnp.sum(diag_col * eye, 0, keepdims=True)
    fr = off_r + diag_col * eye
    fi = off_i
    comm_r = dot(fr, gr) - dot(fi, gi) - dot(gr, fr) + dot(gi, fi)
    comm_i = dot(fr, gi) + dot(fi, gr) - dot(gr, fi) - dot(gi, fr)
    d1_r[...] = comm_i + cr + cr.T
    d1_i[...] = ci - ci.T - comm_r

    from_cols = jnp.zeros((1, 256), F32)
    lane_group = iota((1, 256), 1) // 64
    row64 = iota((64, 64), 0)
    table = coup[...] + diag_col + diag_row
    table_wide = dot(table, repeat)
    row_wide = iota((64, 256), 0)
    for k in range(COLS):
        picked = jnp.sum(
            jnp.where(row_wide == cb * COLS + k, table_wide, 0.0), 0, keepdims=True
        )
        from_cols = jnp.where(lane_group == k, picked, from_cols)
    table_t = coup_t + diag_col + diag_row
    for i in range(ROWS):
        from_rows = jnp.sum(
            jnp.where(iota((64, 64), 1) == rb * ROWS + i, table_t, 0.0), 1, keepdims=True
        )
        rows = slice(i * 64, i * 64 + 64)
        factor = from_rows - from_cols
        out_r[rows, :] += factor * g2i[rows, :]
        out_i[rows, :] -= factor * g2r[rows, :]

    for ch in range(2):
        for g in range(2):
            sums[ch, g].wait_recv()
            lanes = slice(g * 128, g * 128 + 128)
            for comp in range(2):
                for ip in range(2):
                    cut = slice(ip * 128, ip * 128 + 128)
                    even, odd = half_swap(
                        part[ch, g, comp, 0:64, cut] + part_in[ch, g, comp, 0:64, cut],
                        part[ch, g, comp, 64:128, cut] + part_in[ch, g, comp, 64:128, cut],
                        lower,
                    )
                    top = ch * 256 + ip * 128
                    for first, value in ((top, even), (top + 64, odd)):
                        if comp == 0:
                            out_i[first : first + 64, lanes] -= value
                        else:
                            out_r[first : first + 64, lanes] += value
    for copy in sent:
        copy.wait_send()


def on_device(g2_re, g2_im, g1_re, g1_im, hop_re, hop_im, coupling):
    vmem = pl.BlockSpec(memory_space=pltpu.VMEM)
    smem = pl.BlockSpec(memory_space=pltpu.SMEM)
    count = 72
    return pl.pallas_call(
        kernel,
        out_shape=(
            jax.ShapeDtypeStruct((512, 256), F32),
            jax.ShapeDtypeStruct((512, 256), F32),
            jax.ShapeDtypeStruct((64, 64), F32),
            jax.ShapeDtypeStruct((64, 64), F32),
        ),
        in_specs=[vmem] * 7 + [smem] * 2,
        out_specs=(vmem,) * 4,
        scratch_shapes=[
            pltpu.VMEM((8, 2, 8, 64, 256), F32),
            pltpu.VMEM((8, 2, 2, 256, 256), F32),
            pltpu.VMEM((2, 2, 128, 256), F32),
            pltpu.VMEM((8, 2, 1536, 256), BF16),
            pltpu.VMEM((8, 512, 1024), BF16),
            pltpu.VMEM((2, 4, 2, 128, 256), F32),
            pltpu.VMEM((2, 2, 2, 128, 256), F32),
            pltpu.VMEM((4, 16, 128), F32),
            pltpu.VMEM((4, 16, 128), F32),
            pltpu.VMEM((2, 4, 16, 128), F32),
            pltpu.VMEM((2, 64, 512), F32),
            pltpu.VMEM((2, 256, 256), F32),
            pltpu.VMEM((64, 256), F32),
            pltpu.SemaphoreType.DMA((count,)),
            pltpu.SemaphoreType.DMA((count,)),
        ],
        compiler_params=pltpu.CompilerParams(
            collective_id=0, has_side_effects=True, vmem_limit_bytes=56 * 2**20
        ),
    )(g2_re, g2_im, g1_re.T, g1_im.T, hop_re, hop_im, coupling, hop_re, hop_im)


def solution(mesh):
    pairs = P("prow", ("pcol", "orb"))
    return jax.shard_map(
        on_device,
        mesh=mesh,
        in_specs=(pairs, pairs, pairs, pairs, P(), P(), P()),
        out_specs=(pairs, pairs, P(), P()),
        check_vma=False,
    )
```

time: 129 us -> 97.6 us (0.76)
  the two profiles are of different devices: /device:TPU:0 before, /device:TPU:1 now
where the time goes in v2:
time: 97.6 us; the launch traced here: 97.3 us
  Pallas kernels  92.5 us (95%)
  local copies, waits for them, and re-layouts  4.11 us (4%)
    pallas_call x1, Pallas kernels, on_device(): pl.pallas_call(kernel, out_shape=(jax.ShapeDtypeStruct((512, 256), F32),...  92.5 us
    unnamed x10, local copies, waits for them, and re-layouts  4.11 us

profile of v2, /device:TPU:1, one launch (start us, length us, event | category | flops | bytes accessed | tf_op | source)
XLA Modules:
  0.0 97.3 jit_solution(5301086841198891976)
XLA Ops:
  0.6 92.5 %shard_map.102 = (f32[512,256]{1,0:T(8,128)}, f32[512,256]{1,0:T(8,128)}, f32[64,64]{1,0:T(8,128)}, f32[64,64]{1,0:T(8,128)}) custom-call(f32[512,256]{1,0:T(8,128)} %g2r.1, f32[512,256]{1,0:T(8,128)} %g2i.1, f32[4,8]{1,0:T(4,128)} %bitcast.2, f32[4,8]{1,0:T(4,128)} %bitcast.3, f32[64,64]{1,0:T(8,128)} %hop_r_s.1, f32[64,64]{1,0:T(8,128)} %hop_i_s.1, ...), custom_call_target="tpu_custom_call" | custom-call | tf_op jit(solution)/shard_map/pallas_call | solution.py:529
  93.1 0.0 copy-start
  93.2 1.9 %copy.15 = f32[512,256]{1,0:T(8,128)} copy(f32[512,256]{1,0:T(8,128)} %get-tuple-element.8) | data formatting | bytes 1048576
  95.1 0.0 copy-done
  95.1 0.0 copy-start.2
  95.1 0.8 copy.16
  95.9 0.0 copy-done.2
  95.9 0.0 copy-start.1
  95.9 0.6 copy.17
  96.5 0.2 copy-done.1
  96.7 0.6 copy.18
Async XLA Ops:
  93.1 1.9 %copy-start = (f32[512,256]{1,0:T(8,128)S(1)}, f32[512,256]{1,0:T(8,128)}, u32[]{:S(2)}) copy-start(f32[512,256]{1,0:T(8,128)} %get-tuple-element.9) | copy-start | bytes 1572868
  95.1 0.8 copy-start.2
  95.9 0.8 copy-start.1

commit v3 on v2

--- a/solution.py
+++ b/solution.py
@@ -161,7 +161,7 @@
         go(6, 0, ch, first, last, at(dx=1))
         go(2, 0, ch, first, last, at(dx=3))
 
-    own_y(0, 0, 3)
+    own_y(0, 0, 4)
     own_x(0, 6, 8)
     own_x(0, 0, 6)
     pre = [
@@ -171,7 +171,7 @@
     z_first = {}
     for d, name in ((1, "m"), (3, "p")):
         z_first[name, 0] = push(left.at[rb, 0], left.at[rb, 0], at(dz=d))
-    own_y(0, 3, 6)
+    own_y(0, 4, 6)
     own_y(0, 6, 8)
     own_x(1, 6, 8)
     sib = {(0, 0): push(left.at[rb, 0], left.at[rb, 0], at(dc=1))}
@@ -224,10 +224,10 @@
         for g in range(4):
             part[ch, g] = jnp.zeros((2, 128, 256), F32)
 
-    def prepare(slot, ch):
+    def prepare(slot, ch, parts):
         base = col_block(*where_is(slot)) * COLS
         match = iota((64, 256), 0) == iota((64, 256), 1) % 64
-        for a in range(4):
+        for a in parts:
             v = jnp.sum(
                 jnp.where(iota((64, 64), 1) == base + a, coup_t, 0.0), 1, keepdims=True
             )
@@ -243,23 +243,23 @@
                     if comp == 1:
                         stack[slot, ch, row + 512 : row + 576, :] = -term
 
-    def mix(slot, ch):
+    def mix(slot, ch, parts):
         base = col_block(*where_is(slot)) * COLS
         starts = (cb * COLS, col_block(x, ya) * COLS, col_block(x, yb) * COLS)
         for kk in range(8):
             k = starts[0] + kk if kk < 4 else starts[1 if kk < 6 else 2] + kk - 4
-            scale = []
-            for a in range(4):
+            scale = {}
+            for a in parts:
                 sr = 0.5 * (hop_r_s[base + a, k] + hop_r_s[k, base + a])
                 si = 0.5 * (hop_i_s[base + a, k] - hop_i_s[k, base + a])
                 sr = jnp.where(k == base + a, 0.0, sr)
-                scale.append((jnp.full((8, 256), sr, F32), jnp.full((8, 256), si, F32)))
+                scale[a] = jnp.full((8, 256), sr, F32), jnp.full((8, 256), si, F32)
             for strip in range(8):
                 to = slice((kk % 2) * 64 + strip * 8, (kk % 2) * 64 + strip * 8 + 8)
                 rows = slice(strip * 8, strip * 8 + 8)
                 acc_r = part[ch, kk // 2, 0, to, :]
                 acc_i = part[ch, kk // 2, 1, to, :]
-                for a in range(4):
+                for a in parts:
                     sr, si = scale[a]
                     tr = right[slot, ch, 2 * a, rows, :]
                     ti = right[slot, ch, 2 * a + 1, rows, :]
@@ -268,11 +268,11 @@
                 part[ch, kk // 2, 0, to, :] = acc_r
                 part[ch, kk // 2, 1, to, :] = acc_i
 
-    def enter(ch, first, count=1, stride=1):
+    def enter(ch, first, count=1, stride=1, parts=(0, 1, 2, 3)):
         @pl.loop(0, count)
         def _(n):
-            prepare(first + n * stride, ch)
-            mix(first + n * stride, ch)
+            prepare(first + n * stride, ch, parts)
+            mix(first + n * stride, ch, parts)
 
     def split_left(which, p):
         @pl.loop(0, 4)
@@ -307,20 +307,23 @@
 
     def along_x(ch, first):
         arrived(1, ch, first)
-        go(7, 1, ch, first, first + 3, at(dx=1))
-        go(3, 1, ch, first, first + 3, at(dx=3))
-
-    def relay_few(ch):
+        go(7, 1, ch, first, 4 + first // 2, at(dx=1))
+        go(3, 1, ch, first, 4 + first // 2, at(dx=3))
+
+    def relay_few_x(ch):
         arrived(6, ch, 6)
         arrived(2, ch, 6)
         go(4, 6, ch, 6, 7, at(dx=1))
         go(4, 2, ch, 7, 8, at(dx=3))
+
+    def relay_few_y(ch):
         go(7, 6, ch, 6, 8, at(dy=2))
         go(3, 2, ch, 6, 8, at(dy=2))
 
     def relay(ch):
         arrived(6, ch, 0)
-        go(4, 6, ch, 0, 6, at(dx=1))
+        go(4, 6, ch, 0, 4, at(dx=1))
+        go(4, 6, ch, 4, 6, at(dx=1))
         arrived(2, ch, 0)
 
     def relay_far(ch):
@@ -329,7 +332,7 @@
 
     def relay_last(ch, first):
         arrived(3, ch, first)
-        go(5, 3, ch, first, first + 3, at(dx=3))
+        go(5, 3, ch, first, 4 + first // 2, at(dx=3))
 
     rb_m = ((z + 3) % 4) * 2 + c
     rb_p = ((z + 1) % 4) * 2 + c
@@ -355,10 +358,14 @@
             sib[dz, p].wait_recv()
             split_left(((z + dz) % 4) * 2 + 1 - c, p)
 
-    def by_left(dz):
-        @pl.loop(0, 2)
-        def _(cc):
-            multiply(slot_of((z + dz) % 4, cc), 0)
+    def by_left(first, count, far):
+        @pl.loop(0, count)
+        def _(n):
+            slot = slot_of((z + 3 + (first + n) // 2) % 4, n % 2)
+
+            @pl.when((slot // 2 == 2) == far)
+            def _():
+                multiply(slot, 0)
 
     def times(first, count, stride, halves=(0, 1)):
         @pl.loop(0, count)
@@ -371,97 +378,105 @@
         sums[ch, 0] = push(part.at[ch, 2], part_in.at[ch, 0], dev_a)
         sums[ch, 1] = push(part.at[ch, 3], part_in.at[ch, 1], dev_b)
 
+    relay_few_x(0)
+    relay_few_y(0)
+    enter(0, 0)
     along_x(0, 0)
-    enter(0, 0)
+    enter(1, 0)
+    split_left(rb, 0)
+
+    for half in range(2):
+        rows = slice(half * 256, half * 256 + 256)
+        gr, gi = g2r[rows, :], g2i[rows, :]
+        kr, ki = kron[0], kron[1]
+        out_r[rows, :] = dot(kr, gi) + dot(ki, gr) - dot(gr, ki) - dot(gi, kr)
+        out_i[rows, :] = dot(ki, gi) - dot(kr, gr) + dot(gr, kr) - dot(gi, ki)
+
     for copy in pre:
         copy.wait_recv()
     for d, name in ((1, "m"), (3, "p")):
         z_first[name, 1] = push(left.at[rb, 1], left.at[rb, 1], at(dz=d))
     sib[0, 1] = push(left.at[rb, 1], left.at[rb, 1], at(dc=1))
-    relay_few(0)
+    pass_on(0)
+    split_left(rb, 1)
+    along_x(0, 4)
     relay(0)
-    along_x(0, 3)
-    pass_on(0)
-    own_y(1, 0, 3)
-    own_y(1, 3, 6)
+    relay_far(0)
+    own_y(1, 0, 4)
+    own_y(1, 4, 6)
+    relay_few_x(1)
+    relay_few_y(1)
     own_y(1, 6, 8)
+    split_left(rb_m, 0)
+    split_left(rb_p, 0)
+    arrived(1, 0, 6)
+    enter(0, 1)
+    enter(0, 2, 2, 4)
+    relay_last(0, 0)
     for copy in tiny_y:
         copy.wait_recv()
     small_x[0] = small_y[0] + small_y[1] + small_y[2] + small_y[3]
     tiny_x = [
         push(small_x.at[0], small_x.at[n], at(dx=d)) for n, d in ((1, 1), (2, 3), (3, 2))
     ]
-    split_left(rb, 0)
-    split_left(rb, 1)
-    split_left(rb_m, 0)
-    split_left(rb_p, 0)
-    arrived(1, 0, 6)
-    enter(0, 1)
-    relay_last(0, 0)
-    enter(0, 2, 2, 4)
-    relay_last(0, 3)
+    relay_last(0, 4)
     own_x(1, 0, 6)
-    relay_far(0)
+    arrived(3, 0, 6)
+    arrived(7, 0, 0, 4, 6)
+    enter(0, 3, 2, 4)
     pass_on(1)
+    from_sibling(0)
+    split_left(rb_m, 1)
+    split_left(rb_p, 1)
+    from_sibling(3)
+    from_sibling(1)
+    by_left(0, 6, False)
+    along_x(1, 0)
+    along_x(1, 4)
+    relay_far(1)
+    arrived(4, 0, 0, 4)
+    arrived(5, 0, 0, 4, 6)
+    enter(0, 4, 2)
+    by_left(0, 6, True)
     for copy in tiny_x:
         copy.wait_recv()
     small_z[c, z] = small_x[0] + small_x[1] + small_x[2] + small_x[3]
     tiny_z = [
         push(small_z.at[c, z], small_z.at[c, z], at(dz=d)) for d in (1, 3, 2)
     ]
-    along_x(1, 0)
-    along_x(1, 3)
-    split_left(rb_m, 1)
-    split_left(rb_p, 1)
-    arrived(3, 0, 6)
-    arrived(7, 0, 0, 3, 6)
-    enter(0, 3, 2, 4)
-    from_sibling(0)
-    enter(1, 0)
+    pass_far(0)
+    pass_far(1)
+    from_sibling(2)
+    by_left(6, 2, False)
+    by_left(6, 2, True)
+    send_sums(0)
+    relay(1)
     arrived(1, 1, 6)
     enter(1, 1)
-    pass_far(0)
-    from_sibling(3)
-    from_sibling(1)
-    arrived(4, 0, 0)
-    arrived(5, 0, 0, 3, 6)
-    enter(0, 4, 2)
-    by_left(0)
-    by_left(3)
-    by_left(1)
-    for copy in tiny_z:
-        copy.wait_recv()
-    tiny_c = push(small_z.at[c], small_z.at[c], at(dc=1))
-    pass_far(1)
-    from_sibling(2)
-    by_left(2)
-    send_sums(0)
-    relay_few(1)
-    relay(1)
     enter(1, 2, 2, 4)
     times(0, 2, 1)
     relay_last(1, 0)
     times(2, 2, 4)
-    relay_last(1, 3)
-    relay_far(1)
+    relay_last(1, 4)
+    for copy in tiny_z:
+        copy.wait_recv()
+    tiny_c = push(small_z.at[c], small_z.at[c], at(dc=1))
     arrived(3, 1, 6)
-    arrived(7, 1, 0, 3, 6)
+    arrived(7, 1, 0, 4, 6)
     enter(1, 3, 2, 4)
     times(3, 2, 4)
+    arrived(5, 1, 6)
+    enter(1, 4, 2, parts=(3,))
     arrived(4, 1, 0)
-    arrived(5, 1, 0, 3, 6)
-    enter(1, 4, 2)
+    arrived(5, 1, 0)
+    enter(1, 4, 2, parts=(0, 1))
+    arrived(4, 1, 4)
+    arrived(5, 1, 4)
+    enter(1, 4, 2, parts=(2,))
     times(4, 2, 1, (1,))
     send_sums(1)
     times(4, 2, 1, (0,))
     tiny_c.wait_recv()
-
-    for half in range(2):
-        rows = slice(half * 256, half * 256 + 256)
-        gr, gi = g2r[rows, :], g2i[rows, :]
-        kr, ki = kron[0], kron[1]
-        out_r[rows, :] = dot(kr, gi) + dot(ki, gr) - dot(gr, ki) - dot(gi, kr)
-        out_i[rows, :] = dot(ki, gi) - dot(kr, gr) + dot(gr, kr) - dot(gi, ki)
 
     rows_z = [(r // 2, r % 2) for r in range(8)]
     one = jnp.concatenate([small_z[cc, zz, 0:8, :] for zz, cc in rows_z], 0)
@@ -522,18 +537,24 @@
         copy.wait_send()
 
 
+def finish(a, b, c, d, out_a, out_b, out_c, out_d):
+    for src, dst in ((a, out_a), (b, out_b), (c, out_c), (d, out_d)):
+        dst[...] = src[...]
+
+
 def on_device(g2_re, g2_im, g1_re, g1_im, hop_re, hop_im, coupling):
     vmem = pl.BlockSpec(memory_space=pltpu.VMEM)
     smem = pl.BlockSpec(memory_space=pltpu.SMEM)
     count = 72
-    return pl.pallas_call(
+    shapes = (
+        jax.ShapeDtypeStruct((512, 256), F32),
+        jax.ShapeDtypeStruct((512, 256), F32),
+        jax.ShapeDtypeStruct((64, 64), F32),
+        jax.ShapeDtypeStruct((64, 64), F32),
+    )
+    parts = pl.pallas_call(
         kernel,
-        out_shape=(
-            jax.ShapeDtypeStruct((512, 256), F32),
-            jax.ShapeDtypeStruct((512, 256), F32),
-            jax.ShapeDtypeStruct((64, 64), F32),
-            jax.ShapeDtypeStruct((64, 64), F32),
-        ),
+        out_shape=shapes,
         in_specs=[vmem] * 7 + [smem] * 2,
         out_specs=(vmem,) * 4,
         scratch_shapes=[
@@ -557,6 +578,9 @@
             collective_id=0, has_side_effects=True, vmem_limit_bytes=56 * 2**20
         ),
     )(g2_re, g2_im, g1_re.T, g1_im.T, hop_re, hop_im, coupling, hop_re, hop_im)
+    return pl.pallas_call(
+        finish, out_shape=shapes, in_specs=[vmem] * 4, out_specs=(vmem,) * 4
+    )(*parts)
 
 
 def solution(mesh):

time: 97.6 us -> 85.2 us (0.87)
  the two profiles are of different devices: /device:TPU:1 before, /device:TPU:0 now
where the time goes in v3:
time: 85.2 us; the launch traced here: 84.6 us
  Pallas kernels  83.9 us (98%)
    pallas_call x1, Pallas kernels, on_device(): pl.pallas_call(kernel, out_shape=shapes, in_specs=[vmem] * 7 + [smem] * 2...  81.7 us
    pallas_call x1, Pallas kernels, on_device(): pl.pallas_call(finish, out_shape=shapes, in_specs=[vmem] * 4, out_specs=(...  2.21 us

profile of v3, /device:TPU:0, one launch (start us, length us, event | category | flops | bytes accessed | tf_op | source)
XLA Modules:
  0.0 84.6 jit_solution(10253643852034686189)
XLA Ops:
  0.6 81.7 %shard_map.102 = (f32[512,256]{1,0:T(8,128)}, f32[512,256]{1,0:T(8,128)}, f32[64,64]{1,0:T(8,128)}, f32[64,64]{1,0:T(8,128)}) custom-call(f32[512,256]{1,0:T(8,128)} %g2r.1, f32[512,256]{1,0:T(8,128)} %g2i.1, f32[4,8]{1,0:T(4,128)} %bitcast.2, f32[4,8]{1,0:T(4,128)} %bitcast.3, f32[64,64]{1,0:T(8,128)} %hop_r_s.1, f32[64,64]{1,0:T(8,128)} %hop_i_s.1, ...), custom_call_target="tpu_custom_call" | custom-call | tf_op jit(solution)/shard_map/pallas_call | solution.py:555
  82.4 2.2 %shard_map.103 = (f32[512,256]{1,0:T(8,128)}, f32[512,256]{1,0:T(8,128)}, f32[64,64]{1,0:T(8,128)}, f32[64,64]{1,0:T(8,128)}) custom-call(f32[512,256]{1,0:T(8,128)} %get-tuple-element.8.a, f32[512,256]{1,0:T(8,128)} %get-tuple-element.9.b, f32[64,64]{1,0:T(8,128)} %get-tuple-element.10.c, f32[64,64]{1,0:T(8,128)} %get-tuple-element.11.d), custom_call_target="tpu_custom_call" | custom-call | tf_op jit(solution)/shard_map/pallas_call | solution.py:581

commit v4 on v3

--- a/solution.py
+++ b/solution.py
@@ -146,13 +146,18 @@
 
     got = {}
 
-    def go(to, start, ch, first, last, device):
+    whole = pl.ds(0, 256)
+    sides = pl.ds(0, 128), pl.ds(128, 128)
+
+    def go(to, start, ch, first, last, device, lanes=whole):
         cut = pl.ds(first, last - first)
-        got[to, ch, first] = push(right.at[start, ch, cut], right.at[to, ch, cut], device)
-
-    def arrived(slot, ch, *firsts):
+        got[to, ch, first, lanes.start] = push(
+            right.at[start, ch, cut, :, lanes], right.at[to, ch, cut, :, lanes], device
+        )
+
+    def arrived(slot, ch, *firsts, lanes=whole):
         for first in firsts:
-            got[slot, ch, first].wait_recv()
+            got[slot, ch, first, lanes.start].wait_recv()
 
     def own_y(ch, first, last):
         go(1, 0, ch, first, last, at(dy=2))
@@ -224,26 +229,28 @@
         for g in range(4):
             part[ch, g] = jnp.zeros((2, 128, 256), F32)
 
-    def prepare(slot, ch, parts):
+    def prepare(slot, ch, parts, lanes):
         base = col_block(*where_is(slot)) * COLS
-        match = iota((64, 256), 0) == iota((64, 256), 1) % 64
+        match = iota((64, lanes.size), 0) == iota((64, lanes.size), 1) % 64
         for a in parts:
             v = jnp.sum(
                 jnp.where(iota((64, 64), 1) == base + a, coup_t, 0.0), 1, keepdims=True
             )
             for comp in range(2):
-                value = v * right[slot, ch, 2 * a + comp] + jnp.where(
+                value = v * right[slot, ch, 2 * a + comp, :, lanes] + jnp.where(
                     match,
-                    field_rows[comp, pl.ds(base + a, 1), ch * 256 : ch * 256 + 256],
+                    field_rows[comp, pl.ds(base + a, 1), ch * 256 : ch * 256 + 256][
+                        :, lanes.start : lanes.start + lanes.size
+                    ],
                     0.0,
                 )
                 for n, term in enumerate(split(value)):
                     row = n * 768 + (1 - comp) * 256 + a * 64
-                    stack[slot, ch, row : row + 64, :] = term
+                    stack[slot, ch, row : row + 64, lanes] = term
                     if comp == 1:
-                        stack[slot, ch, row + 512 : row + 576, :] = -term
-
-    def mix(slot, ch, parts):
+                        stack[slot, ch, row + 512 : row + 576, lanes] = -term
+
+    def mix(slot, ch, parts, lanes):
         base = col_block(*where_is(slot)) * COLS
         starts = (cb * COLS, col_block(x, ya) * COLS, col_block(x, yb) * COLS)
         for kk in range(8):
@@ -253,26 +260,26 @@
                 sr = 0.5 * (hop_r_s[base + a, k] + hop_r_s[k, base + a])
                 si = 0.5 * (hop_i_s[base + a, k] - hop_i_s[k, base + a])
                 sr = jnp.where(k == base + a, 0.0, sr)
-                scale[a] = jnp.full((8, 256), sr, F32), jnp.full((8, 256), si, F32)
+                scale[a] = tuple(jnp.full((8, lanes.size), f, F32) for f in (sr, si))
             for strip in range(8):
                 to = slice((kk % 2) * 64 + strip * 8, (kk % 2) * 64 + strip * 8 + 8)
                 rows = slice(strip * 8, strip * 8 + 8)
-                acc_r = part[ch, kk // 2, 0, to, :]
-                acc_i = part[ch, kk // 2, 1, to, :]
+                acc_r = part[ch, kk // 2, 0, to, lanes]
+                acc_i = part[ch, kk // 2, 1, to, lanes]
                 for a in parts:
                     sr, si = scale[a]
-                    tr = right[slot, ch, 2 * a, rows, :]
-                    ti = right[slot, ch, 2 * a + 1, rows, :]
+                    tr = right[slot, ch, 2 * a, rows, lanes]
+                    ti = right[slot, ch, 2 * a + 1, rows, lanes]
                     acc_r += si * ti - sr * tr
                     acc_i -= sr * ti + si * tr
-                part[ch, kk // 2, 0, to, :] = acc_r
-                part[ch, kk // 2, 1, to, :] = acc_i
-
-    def enter(ch, first, count=1, stride=1, parts=(0, 1, 2, 3)):
+                part[ch, kk // 2, 0, to, lanes] = acc_r
+                part[ch, kk // 2, 1, to, lanes] = acc_i
+
+    def enter(ch, first, count=1, stride=1, parts=(0, 1, 2, 3), lanes=whole):
         @pl.loop(0, count)
         def _(n):
-            prepare(first + n * stride, ch, parts)
-            mix(first + n * stride, ch, parts)
+            prepare(first + n * stride, ch, parts, lanes)
+            mix(first + n * stride, ch, parts, lanes)
 
     def split_left(which, p):
         @pl.loop(0, 4)
@@ -284,23 +291,21 @@
                     lane = n * 512 + comp * 256
                     lsplit[which, to, lane : lane + 256] = term
 
-    def multiply(slot, ch, halves=(0, 1)):
+    def multiply(slot, ch, halves=(0, 1), lanes=whole):
         xx, yy = where_is(slot)
         which = (yy // 2) * 4 + xx
         rows = slice(halves[0] * 256, halves[-1] * 256 + 256)
-
-        @pl.loop(0, 2)
-        def _(comp):
+        for comp in range(2):
             start = (1 - comp) * 256
-            high = stack[slot, ch, pl.ds(pl.multiple_of(start, 256), 512), :]
-            low = stack[slot, ch, pl.ds(pl.multiple_of(start + 768, 256), 512), :]
+            high = stack[slot, ch, start : start + 512, lanes]
+            low = stack[slot, ch, start + 768 : start + 1280, lanes]
             value = (
                 mxu(lsplit[which, rows, 0:512], high)
                 + mxu(lsplit[which, rows, 0:512], low)
                 + mxu(lsplit[which, rows, 512:1024], high)
             )
             for n in range(2 * len(halves)):
-                part[ch, 2 * halves[0] + n, comp] += value[n * 128 : n * 128 + 128]
+                part[ch, 2 * halves[0] + n, comp, :, lanes] += value[n * 128 : n * 128 + 128]
 
     def slot_of(zz, cc):
         return ((2 * (zz % 2) + cc - x + 4) % 4) * 2 + (zz // 2 + y // 2) % 2
@@ -309,6 +314,12 @@
         arrived(1, ch, first)
         go(7, 1, ch, first, 4 + first // 2, at(dx=1))
         go(3, 1, ch, first, 4 + first // 2, at(dx=3))
+
+    def along_x_sides():
+        arrived(1, 1, 0, 4)
+        for lanes in sides:
+            go(7, 1, 1, 0, 6, at(dx=1), lanes)
+            go(3, 1, 1, 0, 6, at(dx=3), lanes)
 
     def relay_few_x(ch):
         arrived(6, ch, 6)
@@ -322,8 +333,12 @@
 
     def relay(ch):
         arrived(6, ch, 0)
-        go(4, 6, ch, 0, 4, at(dx=1))
-        go(4, 6, ch, 4, 6, at(dx=1))
+        if ch == 0:
+            go(4, 6, 0, 0, 6, at(dx=1))
+        else:
+            go(4, 6, 1, 0, 6, at(dx=1), sides[0])
+            go(4, 6, 1, 0, 4, at(dx=1), sides[1])
+            go(4, 6, 1, 4, 6, at(dx=1), sides[1])
         arrived(2, ch, 0)
 
     def relay_far(ch):
@@ -333,6 +348,11 @@
     def relay_last(ch, first):
         arrived(3, ch, first)
         go(5, 3, ch, first, 4 + first // 2, at(dx=3))
+
+    def relay_last_side(n):
+        arrived(3, 1, 0, lanes=sides[n])
+        for first, last in ((0, 6),) if n == 0 else ((0, 4), (4, 6)):
+            go(5, 3, 1, first, last, at(dx=3), sides[n])
 
     rb_m = ((z + 3) % 4) * 2 + c
     rb_p = ((z + 1) % 4) * 2 + c
@@ -367,16 +387,18 @@
             def _():
                 multiply(slot, 0)
 
-    def times(first, count, stride, halves=(0, 1)):
+    def times(first, count, stride, halves=(0, 1), lanes=whole):
         @pl.loop(0, count)
         def _(n):
-            multiply(first + n * stride, 1, halves)
+            multiply(first + n * stride, 1, halves, lanes)
 
     sums = {}
 
-    def send_sums(ch):
-        sums[ch, 0] = push(part.at[ch, 2], part_in.at[ch, 0], dev_a)
-        sums[ch, 1] = push(part.at[ch, 3], part_in.at[ch, 1], dev_b)
+    def send_sums(ch, lanes=whole):
+        for g, device in enumerate((dev_a, dev_b)):
+            sums[ch, g, lanes.start] = push(
+                part.at[ch, 2 + g, :, :, lanes], part_in.at[ch, g, :, :, lanes], device
+            )
 
     relay_few_x(0)
     relay_few_y(0)
@@ -431,10 +453,9 @@
     from_sibling(3)
     from_sibling(1)
     by_left(0, 6, False)
-    along_x(1, 0)
-    along_x(1, 4)
+    along_x_sides()
     relay_far(1)
-    arrived(4, 0, 0, 4)
+    arrived(4, 0, 0)
     arrived(5, 0, 0, 4, 6)
     enter(0, 4, 2)
     by_left(0, 6, True)
@@ -455,26 +476,33 @@
     enter(1, 1)
     enter(1, 2, 2, 4)
     times(0, 2, 1)
-    relay_last(1, 0)
+    relay_last_side(0)
     times(2, 2, 4)
-    relay_last(1, 4)
+    relay_last_side(1)
     for copy in tiny_z:
         copy.wait_recv()
     tiny_c = push(small_z.at[c], small_z.at[c], at(dc=1))
     arrived(3, 1, 6)
-    arrived(7, 1, 0, 4, 6)
+    arrived(7, 1, 6)
+    for lanes in sides:
+        arrived(7, 1, 0, lanes=lanes)
     enter(1, 3, 2, 4)
     times(3, 2, 4)
     arrived(5, 1, 6)
     enter(1, 4, 2, parts=(3,))
-    arrived(4, 1, 0)
-    arrived(5, 1, 0)
-    enter(1, 4, 2, parts=(0, 1))
-    arrived(4, 1, 4)
-    arrived(5, 1, 4)
-    enter(1, 4, 2, parts=(2,))
-    times(4, 2, 1, (1,))
-    send_sums(1)
+    for slot in (4, 5):
+        arrived(slot, 1, 0, lanes=sides[0])
+    enter(1, 4, 2, 1, (0, 1, 2), sides[0])
+    times(4, 2, 1, (1,), sides[0])
+    send_sums(1, sides[0])
+    for slot in (4, 5):
+        arrived(slot, 1, 0, lanes=sides[1])
+    enter(1, 4, 2, 1, (0, 1), sides[1])
+    for slot in (4, 5):
+        arrived(slot, 1, 4, lanes=sides[1])
+    enter(1, 4, 2, 1, (2,), sides[1])
+    times(4, 2, 1, (1,), sides[1])
+    send_sums(1, sides[1])
     times(4, 2, 1, (0,))
     tiny_c.wait_recv()
 
@@ -517,7 +545,9 @@
 
     for ch in range(2):
         for g in range(2):
-            sums[ch, g].wait_recv()
+            sums[ch, g, 0].wait_recv()
+            if ch == 1:
+                sums[1, g, 128].wait_recv()
             lanes = slice(g * 128, g * 128 + 128)
             for comp in range(2):
                 for ip in range(2):
@@ -545,7 +575,7 @@
 def on_device(g2_re, g2_im, g1_re, g1_im, hop_re, hop_im, coupling):
     vmem = pl.BlockSpec(memory_space=pltpu.VMEM)
     smem = pl.BlockSpec(memory_space=pltpu.SMEM)
-    count = 72
+    count = 96
     shapes = (
         jax.ShapeDtypeStruct((512, 256), F32),
         jax.ShapeDtypeStruct((512, 256), F32),

time: 85.2 us -> 82.3 us (0.966)
  Pallas kernels: 83.9 us -> 81.5 us
    pallas_call x1, Pallas kernels: 81.7 us -> 79.3 us  [on_device(): pl.pallas_call(kernel, out_shape=shapes, in_specs=[vmem] * 7 + [smem] * 2...]
where the time goes in v4:
time: 82.3 us; the launch traced here: 82.1 us
  Pallas kernels  81.5 us (99%)
    pallas_call x1, Pallas kernels, on_device(): pl.pallas_call(kernel, out_shape=shapes, in_specs=[vmem] * 7 + [smem] * 2...  79.3 us
    pallas_call x1, Pallas kernels, on_device(): pl.pallas_call(finish, out_shape=shapes, in_specs=[vmem] * 4, out_specs=(...  2.21 us

profile of v4, /device:TPU:0, one launch (start us, length us, event | category | flops | bytes accessed | tf_op | source)
XLA Modules:
  0.0 82.1 jit_solution(14304172685706201631)
XLA Ops:
  0.6 79.3 %shard_map.102 = (f32[512,256]{1,0:T(8,128)}, f32[512,256]{1,0:T(8,128)}, f32[64,64]{1,0:T(8,128)}, f32[64,64]{1,0:T(8,128)}) custom-call(f32[512,256]{1,0:T(8,128)} %g2r.1, f32[512,256]{1,0:T(8,128)} %g2i.1, f32[4,8]{1,0:T(4,128)} %bitcast.2, f32[4,8]{1,0:T(4,128)} %bitcast.3, f32[64,64]{1,0:T(8,128)} %hop_r_s.1, f32[64,64]{1,0:T(8,128)} %hop_i_s.1, ...), custom_call_target="tpu_custom_call" | custom-call | tf_op jit(solution)/shard_map/pallas_call | solution.py:585
  79.9 2.2 %shard_map.103 = (f32[512,256]{1,0:T(8,128)}, f32[512,256]{1,0:T(8,128)}, f32[64,64]{1,0:T(8,128)}, f32[64,64]{1,0:T(8,128)}) custom-call(f32[512,256]{1,0:T(8,128)} %get-tuple-element.8.a, f32[512,256]{1,0:T(8,128)} %get-tuple-element.9.b, f32[64,64]{1,0:T(8,128)} %get-tuple-element.10.c, f32[64,64]{1,0:T(8,128)} %get-tuple-element.11.d), custom_call_target="tpu_custom_call" | custom-call | tf_op jit(solution)/shard_map/pallas_call | solution.py:611

commit v5 on v4

--- a/solution.py
+++ b/solution.py
@@ -450,9 +450,11 @@
     from_sibling(0)
     split_left(rb_m, 1)
     split_left(rb_p, 1)
+    by_left(2, 2, False)
     from_sibling(3)
+    by_left(0, 2, False)
     from_sibling(1)
-    by_left(0, 6, False)
+    by_left(4, 2, False)
     along_x_sides()
     relay_far(1)
     arrived(4, 0, 0)
@@ -467,13 +469,14 @@
     ]
     pass_far(0)
     pass_far(1)
+    enter(1, 1, parts=(0, 1, 2))
     from_sibling(2)
     by_left(6, 2, False)
     by_left(6, 2, True)
     send_sums(0)
     relay(1)
     arrived(1, 1, 6)
-    enter(1, 1)
+    enter(1, 1, parts=(3,))
     enter(1, 2, 2, 4)
     times(0, 2, 1)
     relay_last_side(0)
@@ -567,14 +570,19 @@
         copy.wait_send()
 
 
-def finish(a, b, c, d, out_a, out_b, out_c, out_d):
-    for src, dst in ((a, out_a), (b, out_b), (c, out_c), (d, out_d)):
-        dst[...] = src[...]
+def finish(a, b, c, d, out_a, out_b, out_c, out_d, done):
+    pairs = ((a, out_a), (b, out_b), (c, out_c), (d, out_d))
+    copies = [pltpu.make_async_copy(*pair, done.at[n]) for n, pair in enumerate(pairs)]
+    for copy in copies:
+        copy.start()
+    for copy in copies:
+        copy.wait()
 
 
 def on_device(g2_re, g2_im, g1_re, g1_im, hop_re, hop_im, coupling):
     vmem = pl.BlockSpec(memory_space=pltpu.VMEM)
     smem = pl.BlockSpec(memory_space=pltpu.SMEM)
+    anywhere = pl.BlockSpec(memory_space=pl.ANY)
     count = 96
     shapes = (
         jax.ShapeDtypeStruct((512, 256), F32),
@@ -609,7 +617,11 @@
         ),
     )(g2_re, g2_im, g1_re.T, g1_im.T, hop_re, hop_im, coupling, hop_re, hop_im)
     return pl.pallas_call(
-        finish, out_shape=shapes, in_specs=[vmem] * 4, out_specs=(vmem,) * 4
+        finish,
+        out_shape=shapes,
+        in_specs=[anywhere] * 4,
+        out_specs=(anywhere,) * 4,
+        scratch_shapes=[pltpu.SemaphoreType.DMA((4,))],
     )(*parts)
 
 

time: 82.3 us -> 115 us (1.40)
  Pallas kernels: 81.5 us -> 114 us
    pallas_call x1, Pallas kernels: 2.21 us -> 34.9 us  [on_device(): pl.pallas_call(finish, out_shape=shapes, in_specs=[anywhere] * 4, out_spe...]
where the time goes in v5:
time: 115 us
  Pallas kernels  114 us (99%)
    pallas_call x1, Pallas kernels, on_device(): pl.pallas_call(kernel, out_shape=shapes, in_specs=[vmem] * 7 + [smem] * 2...  79.3 us
    pallas_call x1, Pallas kernels, on_device(): pl.pallas_call(finish, out_shape=shapes, in_specs=[anywhere] * 4, out_spe...  34.9 us

profile of v5, /device:TPU:0, one launch (start us, length us, event | category | flops | bytes accessed | tf_op | source)
XLA Modules:
  0.0 115.0 jit_solution(16492637874114457207)
XLA Ops:
  0.6 79.3 %shard_map.102 = (f32[512,256]{1,0:T(8,128)}, f32[512,256]{1,0:T(8,128)}, f32[64,64]{1,0:T(8,128)}, f32[64,64]{1,0:T(8,128)}) custom-call(f32[512,256]{1,0:T(8,128)} %g2r.1, f32[512,256]{1,0:T(8,128)} %g2i.1, f32[4,8]{1,0:T(4,128)} %bitcast.2, f32[4,8]{1,0:T(4,128)} %bitcast.3, f32[64,64]{1,0:T(8,128)} %hop_r_s.1, f32[64,64]{1,0:T(8,128)} %hop_i_s.1, ...), custom_call_target="tpu_custom_call" | custom-call | tf_op jit(solution)/shard_map/pallas_call | solution.py:593
  79.9 34.9 %shard_map.103 = (f32[512,256]{1,0:T(8,128)}, f32[512,256]{1,0:T(8,128)}, f32[64,64]{1,0:T(8,128)}, f32[64,64]{1,0:T(8,128)}) custom-call(f32[512,256]{1,0:T(8,128)} %get-tuple-element.8.a, f32[512,256]{1,0:T(8,128)} %get-tuple-element.9.b, f32[64,64]{1,0:T(8,128)} %get-tuple-element.10.c, f32[64,64]{1,0:T(8,128)} %get-tuple-element.11.d), custom_call_target="tpu_custom_call" | custom-call | tf_op jit(solution)/shard_map/pallas_call | solution.py:619

commit v6 on v4

--- a/solution.py
+++ b/solution.py
@@ -450,9 +450,11 @@
     from_sibling(0)
     split_left(rb_m, 1)
     split_left(rb_p, 1)
+    by_left(2, 2, False)
     from_sibling(3)
+    by_left(0, 2, False)
     from_sibling(1)
-    by_left(0, 6, False)
+    by_left(4, 2, False)
     along_x_sides()
     relay_far(1)
     arrived(4, 0, 0)
@@ -467,13 +469,14 @@
     ]
     pass_far(0)
     pass_far(1)
+    enter(1, 1, parts=(0, 1, 2))
     from_sibling(2)
     by_left(6, 2, False)
     by_left(6, 2, True)
     send_sums(0)
     relay(1)
     arrived(1, 1, 6)
-    enter(1, 1)
+    enter(1, 1, parts=(3,))
     enter(1, 2, 2, 4)
     times(0, 2, 1)
     relay_last_side(0)

time: 82.3 us -> 82.3 us (level)
  no operation moved by 1% of the time
where the time goes in v6:
time: 82.3 us; the launch traced here: 82.1 us
  Pallas kernels  81.5 us (99%)
    pallas_call x1, Pallas kernels, on_device(): pl.pallas_call(kernel, out_shape=shapes, in_specs=[vmem] * 7 + [smem] * 2...  79.3 us
    pallas_call x1, Pallas kernels, on_device(): pl.pallas_call(finish, out_shape=shapes, in_specs=[vmem] * 4, out_specs=(...  2.21 us

profile of v6, /device:TPU:0, one launch (start us, length us, event | category | flops | bytes accessed | tf_op | source)
XLA Modules:
  0.0 82.1 jit_solution(5315206393814235186)
XLA Ops:
  0.6 79.3 %shard_map.102 = (f32[512,256]{1,0:T(8,128)}, f32[512,256]{1,0:T(8,128)}, f32[64,64]{1,0:T(8,128)}, f32[64,64]{1,0:T(8,128)}) custom-call(f32[512,256]{1,0:T(8,128)} %g2r.1, f32[512,256]{1,0:T(8,128)} %g2i.1, f32[4,8]{1,0:T(4,128)} %bitcast.2, f32[4,8]{1,0:T(4,128)} %bitcast.3, f32[64,64]{1,0:T(8,128)} %hop_r_s.1, f32[64,64]{1,0:T(8,128)} %hop_i_s.1, ...), custom_call_target="tpu_custom_call" | custom-call | tf_op jit(solution)/shard_map/pallas_call | solution.py:588
  79.9 2.2 %shard_map.103 = (f32[512,256]{1,0:T(8,128)}, f32[512,256]{1,0:T(8,128)}, f32[64,64]{1,0:T(8,128)}, f32[64,64]{1,0:T(8,128)}) custom-call(f32[512,256]{1,0:T(8,128)} %get-tuple-element.8.a, f32[512,256]{1,0:T(8,128)} %get-tuple-element.9.b, f32[64,64]{1,0:T(8,128)} %get-tuple-element.10.c, f32[64,64]{1,0:T(8,128)} %get-tuple-element.11.d), custom_call_target="tpu_custom_call" | custom-call | tf_op jit(solution)/shard_map/pallas_call | solution.py:614
